TPU v7x, 32 devices: a whole 2x2x4 slice. The times are simulated.
32 devices in a mesh: section: 2 (over x), dp: 4 (over y, core), mp: 4 (over z).
Axes of the slice: x: 2, y: 2, z: 4, core: 2. Of those that a mesh axis runs over, the one named last changes fastest.
Arguments:
- layer_in: bfloat16 [2, 8, 1024, 512], P('section', 'dp', 'mp'), may hold values from -6 to 6
- segment_ids: int32 [2, 8, 1024], P(None, 'dp'), may hold values from 0 to 3, never falling along the last dimension, each value on 1 to 769 neighbouring positions
- out_grads: bfloat16 [2, 8, 1024, 512], P('section', 'dp', 'mp'), may hold values from -6 to 6
- w_qkv: bfloat16 [2, 512, 3, 512], P('section', 'dp', None, 'mp'), may hold values from -0.25 to 0.25
- w_out: bfloat16 [2, 512, 512], P('section', 'mp', 'dp'), may hold values from -2 to 2
- w_up: bfloat16 [2, 512, 2048], P('section', 'dp', 'mp'), may hold values from -0.25 to 0.25
- w_down: bfloat16 [2, 2048, 512], P('section', 'mp', 'dp'), may hold values from -0.125 to 0.125
- norm_gain: float32 [2, 3, 512], P('section', None, ('dp', 'mp')), may hold values from 0.5 to 1.5
- norm_bias: float32 [2, 3, 512], P('section', None, ('dp', 'mp')), may hold values from -1.2 to 1.2
- w_qc: bfloat16 [512, 512], P('dp', ('section', 'mp')), may hold values from -0.25 to 0.25
- w_kvc: bfloat16 [512, 2, 512], P('dp', None, ('section', 'mp')), may hold values from -0.25 to 0.25
- w_oc: bfloat16 [512, 512], P(('section', 'mp'), 'dp'), may hold values from -2 to 2
Outputs:
- section_out: bfloat16 [2, 8, 1024, 512], P('section', 'dp', 'mp')
- in_grads: bfloat16 [2, 8, 1024, 512], P('section', 'dp', 'mp')
- grad_qkv: float32 [2, 512, 3, 512], P('section', 'dp', None, 'mp')
- grad_out: float32 [2, 512, 512], P('section', 'mp', 'dp')
- grad_up: float32 [2, 512, 2048], P('section', 'dp', 'mp')
- grad_down: float32 [2, 2048, 512], P('section', 'mp', 'dp')
- grad_gain: float32 [2, 3, 512], P('section', None, ('dp', 'mp'))
- grad_bias: float32 [2, 2, 512], P('section', None, ('dp', 'mp'))
- grad_ffn_bias: float32 [2, 512], P('section', ('dp', 'mp'))
- grad_qc: float32 [512, 512], P('dp', ('section', 'mp'))
- grad_kvc: float32 [512, 2, 512], P('dp', None, ('section', 'mp'))
- grad_oc: float32 [512, 512], P(('section', 'mp'), 'dp')
Inputs may be any that keep to these rules, and one draw needn't show every extreme that they name: `segment_ids`: in every row of both layers the segment numbers start at 0 and never fall, all 4 occur, and one segment has 769 positions.
All inputs are finite; a program needn't handle non-finite values.
Results may differ from a plain program's by a relative error of at most 0.035.
Values may be sent and summed in bfloat16 or wider, within the bound.
No kernel may reach another device: no remote copies, remote signals or barrier semaphores. Data moves between devices by JAX's collectives and lax.ppermute only.
A program may use at most 192 MiB of HBM per device.

v0:
```python
from functools import partial

import jax
import jax.numpy as jnp
from jax import lax
from jax.sharding import PartitionSpec as P

HD = 64


EPS = 1e-05
NEG = -1e30
SPAN = 512


def from_partner(block, axis, distance):
    count = lax.axis_size(axis)
    route = []
    for low in range(count):
        high = low | 1 << distance
        if high != low and high < count:
            route += [(low, high), (high, low)]
    return lax.ppermute(block, axis, route)


def shifted(block, axis, distance):
    devices = range(lax.axis_size(axis))
    route = [(i - distance, i) for i in devices if i - distance in devices]
    return lax.ppermute(block, axis, route)


def normalize(states, gain_vec, bias_vec):
    average = jnp.mean(states, axis=-1, keepdims=True)
    centred = states - average
    spread = jnp.mean(centred * centred, axis=-1, keepdims=True)
    return centred * lax.rsqrt(spread + EPS) * gain_vec + bias_vec


def smooth(inputs):
    return jax.nn.gelu(inputs, approximate=False)


def product(left_side, right_side):
    return jnp.dot(left_side, right_side, preferred_element_type=jnp.float32)


def row_product(left_side, right_side, row_start, row_count):
    return product(left_side, right_side)


def pair_product(left_side, left_weight, right_side, right_weight, row_start, row_count):
    return jnp.concatenate(
        [
            row_product(left_side, left_weight, row_start, row_count),
            row_product(right_side, right_weight, row_start, row_count),
        ],
        axis=1,
    )


def gather_rows(row_piece):
    return lax.all_gather(row_piece, "mp", axis=0, tiled=True)


def scatter_rows(term_fn, local_rows):
    return lax.psum_scatter(
        term_fn(jnp.int32(0), local_rows * lax.axis_size("mp")).astype(jnp.bfloat16),
        "mp",
        scatter_dimension=0,
        tiled=True,
    ).astype(jnp.float32)


def masked_scores(queries, key_rows, seg_query, seg_key, factor):
    scores = (
        jnp.einsum("qhe,khe->hqk", queries, key_rows, preferred_element_type=jnp.float32) * factor
    )
    matches = seg_query[:, None] == seg_key[None, :]
    return jnp.where(matches[None], scores, NEG)


def attend(queries, key_rows, value_rows, seg_query, seg_key, factor):
    length, head_count, head_size = queries.shape
    block_rows = min(SPAN, length)
    blocks = length // block_rows

    def one_block(pieces):
        query_block, seg_block = pieces
        scores = masked_scores(query_block, key_rows, seg_block, seg_key, factor)
        highest = jnp.max(scores, axis=-1, keepdims=True)
        weights = jnp.exp(scores - highest)
        totals = jnp.sum(weights, axis=-1, keepdims=True)
        chances = (weights / totals).astype(jnp.bfloat16)
        attended = jnp.einsum(
            "hqk,khe->qhe", chances, value_rows, preferred_element_type=jnp.float32
        )
        return (
            attended.astype(jnp.bfloat16).reshape(block_rows, head_count * head_size),
            (highest + jnp.log(totals))[..., 0],
        )

    attended, log_total = lax.map(
        one_block,
        (
            queries.reshape(blocks, block_rows, head_count, head_size),
            seg_query.reshape(blocks, block_rows),
        ),
    )
    return (attended.reshape(length, head_count * head_size), log_total)


def attend_back(queries, key_rows, value_rows, seg_query, seg_key, log_total, grad_att, factor):
    length, head_count, head_size = queries.shape
    block_rows = min(SPAN, length)
    blocks = length // block_rows

    def one_block(running, pieces):
        query_block, seg_block, total_block, grad_block = pieces
        scores = masked_scores(query_block, key_rows, seg_block, seg_key, factor)
        chances = jnp.exp(scores - total_block[..., None])
        grad_three = grad_block.reshape(block_rows, head_count, head_size)
        d_chances = jnp.einsum(
            "qhe,khe->hqk", grad_three, value_rows, preferred_element_type=jnp.float32
        )
        d_scores = (
            chances * (d_chances - jnp.sum(chances * d_chances, axis=-1, keepdims=True))
        ).astype(jnp.bfloat16)
        d_query = (
            jnp.einsum("hqk,khe->qhe", d_scores, key_rows, preferred_element_type=jnp.float32)
            * factor
        )
        d_keys = (
            running[0]
            + jnp.einsum("hqk,qhe->khe", d_scores, query_block, preferred_element_type=jnp.float32)
            * factor
        )
        d_values = running[1] + jnp.einsum(
            "hqk,qhe->khe",
            chances.astype(jnp.bfloat16),
            grad_three,
            preferred_element_type=jnp.float32,
        )
        return ((d_keys, d_values), d_query.astype(jnp.bfloat16))

    zero_keys = jnp.zeros(key_rows.shape, jnp.float32)
    (d_keys, d_values), d_query = lax.scan(
        one_block,
        (zero_keys, zero_keys),
        (
            queries.reshape(blocks, block_rows, head_count, head_size),
            seg_query.reshape(blocks, block_rows),
            log_total,
            grad_att.reshape(blocks, block_rows, head_count * head_size),
        ),
    )
    return (
        d_query.reshape(length, head_count, head_size),
        d_keys.astype(jnp.bfloat16),
        d_values.astype(jnp.bfloat16),
    )


def on_device(
    layer_in,
    segment_ids,
    out_grads,
    w_qkv,
    w_out,
    w_up,
    w_down,
    norm_gain,
    norm_bias,
    w_qc,
    w_kvc,
    w_oc,
):
    encoder_side = lax.axis_index("section") == 0
    micro_count = layer_in.shape[1]
    local_rows = layer_in.shape[2]
    model_width = layer_in.shape[3]
    seq_length = segment_ids.shape[2]
    factor = HD ** (-0.5)
    fetched = (
        lax.all_gather(w_qkv, "dp", axis=1, tiled=True),
        lax.all_gather(w_out, "dp", axis=2, tiled=True),
        lax.all_gather(w_up, "dp", axis=1, tiled=True),
        lax.all_gather(w_down, "dp", axis=2, tiled=True),
        lax.all_gather(w_qc, "dp", axis=0, tiled=True),
        lax.all_gather(w_kvc, "dp", axis=0, tiled=True),
        lax.all_gather(w_oc, "dp", axis=1, tiled=True),
    )
    qkv_weight = fetched[0][0].reshape(model_width, -1)
    out_weight = fetched[1][0]
    up_weight = fetched[2][0]
    down_weight = fetched[3][0]
    query_weight = fetched[4]
    pair_weight = fetched[5].reshape(model_width, -1)
    cross_weight = fetched[6]
    gains, biases = (
        lax.all_gather(norm_gain, ("dp", "mp"), axis=2, tiled=True),
        lax.all_gather(norm_bias, ("dp", "mp"), axis=2, tiled=True),
    )
    gains = gains[0]
    biases = biases[0]
    source_segs = segment_ids[0]
    target_segs = segment_ids[1]
    own_segs = jnp.where(encoder_side, source_segs, target_segs)
    joined_prev = jnp.zeros((local_rows, model_width), jnp.float32)
    stored = []
    memory_out = []
    decoder_out = []
    for moment in range(micro_count + 1):
        batch_index = min(moment, micro_count - 1)
        start_state = layer_in[0, batch_index].astype(jnp.float32)
        segs_now = own_segs[batch_index]
        normed = normalize(start_state, gains[0], biases[0]).astype(jnp.bfloat16)
        normed_full = gather_rows(normed)
        qkv_now = (
            product(normed_full, qkv_weight).astype(jnp.bfloat16).reshape(seq_length, 3, -1, HD)
        )
        attended, log_total = attend(
            qkv_now[:, 0], qkv_now[:, 1], qkv_now[:, 2], segs_now, segs_now, factor
        )
        mid_state = start_state + scatter_rows(
            partial(row_product, attended, out_weight), local_rows
        )
        ffn_in = jnp.where(encoder_side, mid_state, joined_prev)
        feed_normed = normalize(ffn_in, gains[1], biases[1]).astype(jnp.bfloat16)
        feed_normed_full = gather_rows(feed_normed)
        feed_hidden = smooth(product(feed_normed_full, up_weight)).astype(jnp.bfloat16)
        ffn_out = ffn_in + scatter_rows(partial(row_product, feed_hidden, down_weight), local_rows)
        ffn_kept = feed_normed_full
        third_in = jnp.where(encoder_side, ffn_out, mid_state)
        third_low = normalize(third_in, gains[2], biases[2]).astype(jnp.bfloat16)
        partner = from_partner(third_low, "section", 0)
        pair_rows = jnp.concatenate(
            [
                jnp.where(encoder_side, partner, third_low),
                jnp.where(encoder_side, third_low, partner),
            ],
            axis=1,
        )
        pair_full = gather_rows(pair_rows)
        cross_query = (
            product(pair_full[:, :model_width], query_weight)
            .astype(jnp.bfloat16)
            .reshape(seq_length, -1, HD)
        )
        cross_kv = (
            product(pair_full[:, model_width:], pair_weight)
            .astype(jnp.bfloat16)
            .reshape(seq_length, 2, -1, HD)
        )
        cross_att, cross_log = attend(
            cross_query,
            cross_kv[:, 0],
            cross_kv[:, 1],
            target_segs[batch_index],
            source_segs[batch_index],
            factor,
        )
        cross_part = scatter_rows(partial(row_product, cross_att, cross_weight), local_rows)
        from_encoder = shifted(cross_part.astype(jnp.bfloat16), "section", 1).astype(
            cross_part.dtype
        )
        if moment < micro_count:
            memory_out.append(third_low)
        if moment >= 1:
            decoder_out.append(ffn_out.astype(jnp.bfloat16))
        stored.append(
            (
                start_state,
                mid_state,
                ffn_in,
                third_in,
                normed_full,
                qkv_now,
                attended,
                log_total,
                ffn_kept,
                pair_full,
                cross_query,
                cross_kv,
                cross_att,
                cross_log,
            )
        )
        joined_prev = mid_state + cross_part + from_encoder
    section_out = jnp.stack(
        [
            jnp.where(encoder_side, memory_out[position], decoder_out[position])
            for position in range(micro_count)
        ]
    )[None]
    sums = {
        "qkv": jnp.zeros(qkv_weight.shape, jnp.float32),
        "out": jnp.zeros(out_weight.shape, jnp.float32),
        "up": jnp.zeros(up_weight.shape, jnp.float32),
        "down": jnp.zeros(down_weight.shape, jnp.float32),
        "query": jnp.zeros(query_weight.shape, jnp.float32),
        "pair": jnp.zeros(pair_weight.shape, jnp.float32),
        "cross": jnp.zeros(cross_weight.shape, jnp.float32),
        "gain": jnp.zeros((3, model_width), jnp.float32),
        "bias": jnp.zeros((3, model_width), jnp.float32),
    }

    def feed_backward(states, cotangent, kept_full):
        normed, norm_pull = jax.vjp(normalize, states, gains[1], biases[1])
        cot_low = cotangent.astype(jnp.bfloat16)
        activated, act_pull = jax.vjp(smooth, product(kept_full, up_weight))
        hidden = activated.astype(jnp.bfloat16)
        cot_full = gather_rows(cot_low)
        sums["down"] += product(hidden.T, cot_full)
        d_pre = act_pull(product(cot_full, down_weight.T))[0].astype(jnp.bfloat16)
        sums["up"] += product(kept_full.T, d_pre)
        d_normed = scatter_rows(partial(row_product, d_pre, up_weight.T), local_rows)
        d_state, d_gain, d_bias = norm_pull(d_normed)
        sums["gain"] = sums["gain"].at[1].add(d_gain)
        sums["bias"] = sums["bias"].at[1].add(d_bias)
        return cotangent + d_state

    def self_backward(states, gradient, normed_full, qkv_now, attended, log_total, segs_now):
        _, norm_pull = jax.vjp(normalize, states, gains[0], biases[0])
        grad_full = gather_rows(gradient.astype(jnp.bfloat16))
        sums["out"] += product(attended.T, grad_full)
        d_att = product(grad_full, out_weight.T).astype(jnp.bfloat16)
        d_query, d_keys, d_values = attend_back(
            qkv_now[:, 0],
            qkv_now[:, 1],
            qkv_now[:, 2],
            segs_now,
            segs_now,
            log_total,
            d_att,
            factor,
        )
        d_qkv = jnp.stack([d_query, d_keys, d_values], axis=1).reshape(seq_length, -1)
        sums["qkv"] += product(normed_full.T, d_qkv)
        d_normed = scatter_rows(partial(row_product, d_qkv, qkv_weight.T), local_rows)
        d_state, d_gain, d_bias = norm_pull(d_normed)
        sums["gain"] = sums["gain"].at[0].add(d_gain)
        sums["bias"] = sums["bias"].at[0].add(d_bias)
        return gradient + d_state

    grad_joined = jnp.zeros((local_rows, model_width), jnp.float32)
    input_grads = [None] * micro_count
    for moment in range(micro_count, -1, -1):
        batch_index = min(moment, micro_count - 1)
        live_now = 1.0 if moment < micro_count else 0.0
        live_before = 1.0 if moment >= 1 else 0.0
        (
            start_state,
            mid_state,
            ffn_in,
            third_in,
            self_kept,
            qkv_now,
            attended,
            log_total,
            ffn_kept,
            pair_full,
            cross_query,
            cross_kv,
            cross_att,
            cross_log,
        ) = stored[moment]
        own_grad = jnp.where(encoder_side, 0.0, grad_joined).astype(jnp.bfloat16)
        from_decoder = shifted(own_grad, "section", -1)
        cross_full = gather_rows(jnp.where(encoder_side, from_decoder, own_grad))
        sums["cross"] += product(cross_att.T, cross_full)
        d_cross = product(cross_full, cross_weight.T).astype(jnp.bfloat16)
        d_cq, d_ck, d_cv = attend_back(
            cross_query,
            cross_kv[:, 0],
            cross_kv[:, 1],
            target_segs[batch_index],
            source_segs[batch_index],
            cross_log,
            d_cross,
            factor,
        )
        d_cq = d_cq.reshape(seq_length, -1)
        d_ckv = jnp.stack([d_ck, d_cv], axis=1).reshape(seq_length, -1)
        sums["query"] += product(pair_full[:, :model_width].T, d_cq)
        sums["pair"] += product(pair_full[:, model_width:].T, d_ckv)
        back_parts = scatter_rows(
            partial(pair_product, d_cq, query_weight.T, d_ckv, pair_weight.T), local_rows
        )
        query_part = back_parts[:, :model_width]
        memory_part = back_parts[:, model_width:]
        partner_grad = from_partner(
            jnp.where(encoder_side, query_part, memory_part).astype(jnp.bfloat16), "section", 0
        ).astype(jnp.float32)
        third_grad = (
            jnp.where(
                encoder_side,
                memory_part + out_grads[0, batch_index].astype(jnp.float32) * live_now,
                query_part,
            )
            + partner_grad
        )
        _, third_pull = jax.vjp(normalize, third_in, gains[2], biases[2])
        d_third, d_gain, d_bias = third_pull(third_grad)
        sums["gain"] = sums["gain"].at[2].add(d_gain)
        sums["bias"] = sums["bias"].at[2].add(d_bias)
        ffn_cot = jnp.where(
            encoder_side,
            d_third,
            out_grads[0, max(moment - 1, 0)].astype(jnp.float32) * live_before,
        )
        d_ffn_in = feed_backward(ffn_in, ffn_cot, ffn_kept)
        grad_mid = jnp.where(encoder_side, d_ffn_in, grad_joined + d_third)
        d_start = self_backward(
            start_state, grad_mid, self_kept, qkv_now, attended, log_total, own_segs[batch_index]
        )
        if moment < micro_count:
            input_grads[moment] = d_start.astype(jnp.bfloat16)
        grad_joined = d_ffn_in
    in_grads = jnp.stack(input_grads)[None]
    up_sum, down_sum = (sums["up"], sums["down"])
    reduced = (
        lax.psum_scatter(
            sums["qkv"].reshape(1, model_width, 3, -1).astype(jnp.bfloat16),
            "dp",
            scatter_dimension=1,
            tiled=True,
        ).astype(jnp.float32),
        lax.psum_scatter(
            sums["out"][None].astype(jnp.bfloat16), "dp", scatter_dimension=2, tiled=True
        ).astype(jnp.float32),
        lax.psum_scatter(
            up_sum[None].astype(jnp.bfloat16), "dp", scatter_dimension=1, tiled=True
        ).astype(jnp.float32),
        lax.psum_scatter(
            down_sum[None].astype(jnp.bfloat16), "dp", scatter_dimension=2, tiled=True
        ).astype(jnp.float32),
        lax.psum_scatter(
            sums["query"].astype(jnp.bfloat16), "dp", scatter_dimension=0, tiled=True
        ).astype(jnp.float32),
        lax.psum_scatter(
            sums["pair"].reshape(model_width, 2, -1).astype(jnp.bfloat16),
            "dp",
            scatter_dimension=0,
            tiled=True,
        ).astype(jnp.float32),
        lax.psum_scatter(
            sums["cross"].astype(jnp.bfloat16), "dp", scatter_dimension=1, tiled=True
        ).astype(jnp.float32),
    )
    norm_sums = (
        lax.psum_scatter(sums["gain"][None], ("dp", "mp"), scatter_dimension=2, tiled=True),
        lax.psum_scatter(sums["bias"][None], ("dp", "mp"), scatter_dimension=2, tiled=True),
    )
    bias_total = norm_sums[1]
    bias_attn = jnp.stack([bias_total[:, 0], bias_total[:, 2]], axis=1)
    bias_ffn = bias_total[:, 1]
    return (
        section_out,
        in_grads,
        reduced[0],
        reduced[1],
        reduced[2],
        reduced[3],
        norm_sums[0],
        bias_attn,
        bias_ffn,
        reduced[4],
        reduced[5],
        reduced[6],
    )


def solution(mesh):
    placed = (
        P("section", "dp", "mp", None),
        P(None, "dp", None),
        P("section", "dp", "mp", None),
        P("section", "dp", None, "mp"),
        P("section", "mp", "dp"),
        P("section", "dp", "mp"),
        P("section", "mp", "dp"),
        P("section", None, ("dp", "mp")),
        P("section", None, ("dp", "mp")),
        P("dp", ("section", "mp")),
        P("dp", None, ("section", "mp")),
        P(("section", "mp"), "dp"),
    )
    return jax.shard_map(
        on_device,
        mesh=mesh,
        in_specs=placed,
        out_specs=(
            P("section", "dp", "mp", None),
            P("section", "dp", "mp", None),
            P("section", "dp", None, "mp"),
            P("section", "mp", "dp"),
            P("section", "dp", "mp"),
            P("section", "mp", "dp"),
            P("section", None, ("dp", "mp")),
            P("section", None, ("dp", "mp")),
            P("section", ("dp", "mp")),
            P("dp", ("section", "mp")),
            P("dp", None, ("section", "mp")),
            P(("section", "mp"), "dp"),
        ),
        check_vma=False,
    )
```

profile of v0, /device:TPU:3, one launch (start us, length us, event | category | flops | bytes accessed | tf_op | source)
XLA Modules:
  0.0 1659.1 jit_solution(1042921933986708256)
XLA Ops:
  11.0 31.4 %all_gather.79 = f32[1,3,512]{1,0,2:T(1,128)S(1)} all-gather(f32[1,3,32]{1,0,2:T(1,128)S(1)} %copy.135), channel_id=1, replica_groups=mesh['section'=2,'dp'=4,'mp'=4] {'dp','mp'}, dimensions={2}, use_global_device_ids=true | all-gather | bytes 6528 | tf_op jit(solution)/shard_map/all_gather | solution.py:200
  48.0 30.7 %all_gather.80 = f32[1,3,512]{1,0,2:T(1,128)S(1)} all-gather(f32[1,3,32]{1,0,2:T(1,128)S(1)} %copy.136), channel_id=1, replica_groups=mesh['section'=2,'dp'=4,'mp'=4] {'dp','mp'}, dimensions={2}, use_global_device_ids=true | all-gather | bytes 6528 | tf_op jit(solution)/shard_map/all_gather | solution.py:201
  84.8 9.0 all_gather.83
  93.8 6.8 all_gather.82
  100.6 13.9 all-gather.18.cloned.1.call-done
  116.7 8.6 while.173
  126.9 26.7 %reduce-scatter.40.cloned.1.call-done = bf16[256,512]{1,0:T(8,128)(2,1)} async-done(((bf16[1024,512]{1,0:T(8,128)(2,1)}), bf16[256,512]{1,0:T(8,128)(2,1)}) %reduce-scatter.40.cloned.1.call-update) | async-done | bytes 262160 | tf_op jit(solution)/shard_map/reduce_scatter | solution.py:66
  158.0 7.8 all_gather.85
  165.8 7.3 all_gather.86
  173.1 11.6 all-gather.20.cloned.1.call-done
  184.7 7.5 multiply_convert_fusion.8
  195.0 26.7 %reduce-scatter.42.cloned.1.call-done = bf16[256,512]{1,0:T(8,128)(2,1)} async-done(((bf16[1024,512]{1,0:T(8,128)(2,1)}), bf16[256,512]{1,0:T(8,128)(2,1)}) %reduce-scatter.42.cloned.1.call-update) | async-done | bytes 262160 | tf_op jit(solution)/shard_map/reduce_scatter | solution.py:66
  224.5 6.7 collective-permute-done
  234.7 6.9 all_gather.89
  246.9 6.0 all_gather.90
  255.1 42.9 %all-gather.24.cloned.1.call-done = bf16[1024,1024]{1,0:T(8,128)(2,1)} async-done(((bf16[256,1024]{1,0:T(8,128)(2,1)}), bf16[1024,1024]{1,0:T(8,128)(2,1)}) %all-gather.24.cloned.1.call-update) | async-done | bytes 2097168 | tf_op jit(solution)/shard_map/all_gather | solution.py:62
  301.7 8.3 while.175
  312.4 11.1 while.174
  325.0 12.5 reduce-scatter.46.cloned.1.call-done
  338.8 26.9 %reduce-scatter.44.cloned.1.call-done = bf16[256,512]{1,0:T(8,128)(2,1)} async-done(((bf16[1024,512]{1,0:T(8,128)(2,1)}), bf16[256,512]{1,0:T(8,128)(2,1)}) %reduce-scatter.44.cloned.1.call-update) | async-done | bytes 262160 | tf_op jit(solution)/shard_map/reduce_scatter | solution.py:66
  368.4 26.7 %all-gather.26.cloned.1.call-done = bf16[1024,512]{1,0:T(8,128)(2,1)} async-done(((bf16[256,512]{1,0:T(8,128)(2,1)}), bf16[1024,512]{1,0:T(8,128)(2,1)}) %all-gather.26.cloned.1.call-update) | async-done | bytes 1048592 | tf_op jit(solution)/shard_map/all_gather | solution.py:62
  395.1 7.4 multiply_convert_fusion.7
  405.4 26.7 %reduce-scatter.48.cloned.1.call-done = bf16[256,512]{1,0:T(8,128)(2,1)} async-done(((bf16[1024,512]{1,0:T(8,128)(2,1)}), bf16[256,512]{1,0:T(8,128)(2,1)}) %reduce-scatter.48.cloned.1.call-update) | async-done | bytes 262160 | tf_op jit(solution)/shard_map/reduce_scatter | solution.py:66
  434.1 6.7 collective-permute-done.2
  442.2 45.7 %all-gather.28.cloned.1.call-done = bf16[1024,1024]{1,0:T(8,128)(2,1)} async-done(((bf16[256,1024]{1,0:T(8,128)(2,1)}), bf16[1024,1024]{1,0:T(8,128)(2,1)}) %all-gather.28.cloned.1.call-update) | async-done | bytes 2097168 | tf_op jit(solution)/shard_map/all_gather | solution.py:62
  492.2 8.1 while.176
  501.9 25.8 %reduce-scatter.50.cloned.1.call-done = bf16[256,512]{1,0:T(8,128)(2,1)} async-done(((bf16[1024,512]{1,0:T(8,128)(2,1)}), bf16[256,512]{1,0:T(8,128)(2,1)}) %reduce-scatter.50.cloned.1.call-update) | async-done | bytes 262160 | tf_op jit(solution)/shard_map/reduce_scatter | solution.py:66
  529.0 7.8 collective-permute-done.3
  539.2 27.8 %all-gather.30.cloned.1.call-done = bf16[1024,512]{1,0:T(8,128)(2,1)} async-done(((bf16[256,512]{1,0:T(8,128)(2,1)}), bf16[1024,512]{1,0:T(8,128)(2,1)}) %all-gather.30.cloned.1.call-update) | async-done | bytes 1048592 | tf_op jit(solution)/shard_map/all_gather | solution.py:62
  567.0 7.5 multiply_convert_fusion.6
  585.1 18.9 %reduce-scatter.52.cloned.1.call-done = bf16[256,512]{1,0:T(8,128)(2,1)} async-done(((bf16[1024,512]{1,0:T(8,128)(2,1)}), bf16[256,512]{1,0:T(8,128)(2,1)}) %reduce-scatter.52.cloned.1.call-update) | async-done | bytes 262160 | tf_op jit(solution)/shard_map/reduce_scatter | solution.py:66
  605.9 6.7 collective-permute-done.4
  614.0 18.1 %all-gather.34.cloned.1.call-done = bf16[1024,512]{1,0:T(8,128)(2,1)} async-done(((bf16[256,512]{1,0:T(8,128)(2,1)}), bf16[1024,512]{1,0:T(8,128)(2,1)}) %all-gather.34.cloned.1.call-update) | async-done | bytes 1048592 | tf_op jit(solution)/shard_map/all_gather | solution.py:62
  634.7 44.5 %all-gather.32.cloned.1.call-done = bf16[1024,1024]{1,0:T(8,128)(2,1)} async-done(((bf16[256,1024]{1,0:T(8,128)(2,1)}), bf16[1024,1024]{1,0:T(8,128)(2,1)}) %all-gather.32.cloned.1.call-update) | async-done | bytes 2097168 | tf_op jit(solution)/shard_map/all_gather | solution.py:62
  682.9 6.4 while.177
  690.1 15.5 while.178
  711.2 42.6 %reduce-scatter.54.cloned.1.call-done = bf16[256,1024]{1,0:T(8,128)(2,1)} async-done(((bf16[1024,1024]{1,0:T(8,128)(2,1)}), bf16[256,1024]{1,0:T(8,128)(2,1)}) %reduce-scatter.54.cloned.1.call-update) | async-done | bytes 524304 | tf_op jit(solution)/shard_map/reduce_scatter | solution.py:66
  755.3 6.7 collective-permute-done.6
  764.1 28.5 %all-gather.36.cloned.1.call-done = bf16[1024,512]{1,0:T(8,128)(2,1)} async-done(((bf16[256,512]{1,0:T(8,128)(2,1)}), bf16[1024,512]{1,0:T(8,128)(2,1)}) %all-gather.36.cloned.1.call-update) | async-done | bytes 1048592 | tf_op jit(solution)/shard_map/all_gather | solution.py:62
  799.4 26.7 %reduce-scatter.56.cloned.1.call-done = bf16[256,512]{1,0:T(8,128)(2,1)} async-done(((bf16[1024,512]{1,0:T(8,128)(2,1)}), bf16[256,512]{1,0:T(8,128)(2,1)}) %reduce-scatter.56.cloned.1.call-update) | async-done | bytes 262160 | tf_op jit(solution)/shard_map/reduce_scatter | solution.py:66
  840.2 28.4 %all-gather.38.cloned.1.call-done = bf16[1024,512]{1,0:T(8,128)(2,1)} async-done(((bf16[256,512]{1,0:T(8,128)(2,1)}), bf16[1024,512]{1,0:T(8,128)(2,1)}) %all-gather.38.cloned.1.call-update) | async-done | bytes 1048592 | tf_op jit(solution)/shard_map/all_gather | solution.py:62
  871.1 17.0 %while.179 = (s32[]{:T(128)}, f32[1024,1,64]{0,2,1:T(8,128)}, f32[1024,1,64]{0,2,1:T(8,128)}, bf16[2,512,1,64]{1,3,2,0:T(8,128)(2,1)}, bf16[2,512,1,64]{1,3,2,0:...) while((s32[]{:T(128)}, f32[1024,1,64]{0,2,1:T(8,128)}, ...), condition=%wide.region_54.55_spmd.clone, body=%wide.region_52.54_spmd.clone.sunk | while | flops 341179904 | bytes 17651352 | solution.py:146
  894.6 43.4 %reduce-scatter.58.cloned.1.call-done = bf16[256,1024]{1,0:T(8,128)(2,1)} async-done(((bf16[1024,1024]{1,0:T(8,128)(2,1)}), bf16[256,1024]{1,0:T(8,128)(2,1)}) %reduce-scatter.58.cloned.1.call-update) | async-done | bytes 524304 | tf_op jit(solution)/shard_map/reduce_scatter | solution.py:66
  939.6 6.7 collective-permute-done.8
  948.4 28.5 %all-gather.40.cloned.1.call-done = bf16[1024,512]{1,0:T(8,128)(2,1)} async-done(((bf16[256,512]{1,0:T(8,128)(2,1)}), bf16[1024,512]{1,0:T(8,128)(2,1)}) %all-gather.40.cloned.1.call-update) | async-done | bytes 1048592 | tf_op jit(solution)/shard_map/all_gather | solution.py:62
  983.7 26.7 %reduce-scatter.60.cloned.1.call-done = bf16[256,512]{1,0:T(8,128)(2,1)} async-done(((bf16[1024,512]{1,0:T(8,128)(2,1)}), bf16[256,512]{1,0:T(8,128)(2,1)}) %reduce-scatter.60.cloned.1.call-update) | async-done | bytes 262160 | tf_op jit(solution)/shard_map/reduce_scatter | solution.py:66
  1024.3 28.8 %all-gather.42.cloned.1.call-done = bf16[1024,512]{1,0:T(8,128)(2,1)} async-done(((bf16[256,512]{1,0:T(8,128)(2,1)}), bf16[1024,512]{1,0:T(8,128)(2,1)}) %all-gather.42.cloned.1.call-update) | async-done | bytes 1048592 | tf_op jit(solution)/shard_map/all_gather | solution.py:62
  1055.6 18.3 %while.180 = (s32[]{:T(128)}, f32[1024,1,64]{0,2,1:T(8,128)}, f32[1024,1,64]{0,2,1:T(8,128)}, bf16[2,512,1,64]{1,3,2,0:T(8,128)(2,1)}, bf16[2,512,1,64]{1,3,2,0:...) while((s32[]{:T(128)}, f32[1024,1,64]{0,2,1:T(8,128)}, ...), condition=%wide.region_63.64_spmd.clone, body=%wide.region_61.63_spmd.clone.sunk | while | flops 341179904 | bytes 17651352 | solution.py:146
  1080.6 43.4 %reduce-scatter.62.cloned.1.call-done = bf16[256,1024]{1,0:T(8,128)(2,1)} async-done(((bf16[1024,1024]{1,0:T(8,128)(2,1)}), bf16[256,1024]{1,0:T(8,128)(2,1)}) %reduce-scatter.62.cloned.1.call-update) | async-done | bytes 524304 | tf_op jit(solution)/shard_map/reduce_scatter | solution.py:66
  1125.6 6.7 collective-permute-done.10
  1135.2 27.8 %all-gather.44.cloned.1.call-done = bf16[1024,512]{1,0:T(8,128)(2,1)} async-done(((bf16[256,512]{1,0:T(8,128)(2,1)}), bf16[1024,512]{1,0:T(8,128)(2,1)}) %all-gather.44.cloned.1.call-update) | async-done | bytes 1048592 | tf_op jit(solution)/shard_map/all_gather | solution.py:62
  1179.8 12.6 all-gather.50.cloned.1.call-done
  1194.0 27.3 %reduce-scatter.64.cloned.1.call-done = bf16[256,512]{1,0:T(8,128)(2,1)} async-done(((bf16[1024,512]{1,0:T(8,128)(2,1)}), bf16[256,512]{1,0:T(8,128)(2,1)}) %reduce-scatter.64.cloned.1.call-update) | async-done | bytes 262160 | tf_op jit(solution)/shard_map/reduce_scatter | solution.py:66
  1228.9 31.3 %while.183 = (s32[]{:T(128)}, f32[1024,2,64]{0,2,1:T(8,128)}, f32[1024,2,64]{0,2,1:T(8,128)}, bf16[2,512,2,64]{1,3,2,0:T(8,128)(2,1)}, bf16[2,512,2,64]{1,3,2,0:...) while((s32[]{:T(128)}, f32[1024,2,64]{0,2,1:T(8,128)}, ...), condition=%wide.region_84.85_spmd.clone, body=%wide.region_82.84_spmd.clone.sunk | while | flops 688126976 | bytes 75405640 | solution.py:146
  1288.6 31.3 %while.182 = (s32[]{:T(128)}, f32[1024,2,64]{0,2,1:T(8,128)}, f32[1024,2,64]{0,2,1:T(8,128)}, bf16[2,512,2,64]{1,3,2,0:T(8,128)(2,1)}, bf16[2,512,2,64]{1,3,2,0:...) while((s32[]{:T(128)}, f32[1024,2,64]{0,2,1:T(8,128)}, ...), condition=%wide.region_78.79_spmd.clone, body=%wide.region_76.78_spmd.clone.sunk | while | flops 688126976 | bytes 75405640 | solution.py:146
  1322.3 31.7 %while.181 = (s32[]{:T(128)}, f32[1024,2,64]{0,2,1:T(8,128)}, f32[1024,2,64]{0,2,1:T(8,128)}, bf16[2,512,2,64]{1,3,2,0:T(8,128)(2,1)}, bf16[2,512,2,64]{1,3,2,0:...) while((s32[]{:T(128)}, f32[1024,2,64]{0,2,1:T(8,128)}, ...), condition=%wide.region_72.73_spmd.clone, body=%wide.region_70.72_spmd.clone.sunk | while | flops 688126976 | bytes 80698824 | solution.py:146
  1382.7 22.3 %reduce-scatter.72.cloned.1.call-done = bf16[1,128,512]{2,1,0:T(8,128)(2,1)} async-done(((bf16[1,512,512]{2,1,0:T(8,128)(2,1)}), bf16[1,128,512]{2,1,0:T(8,128)(2,1)}) %reduce-scatter.72.cloned.1.call-update) | async-done | bytes 131088 | tf_op jit(solution)/shard_map/reduce_scatter | solution.py:431
  1406.6 20.4 %reduce-scatter.76.cloned.1.call-done = bf16[128,128]{1,0:T(8,128)(2,1)} async-done(((bf16[512,128]{1,0:T(8,128)(2,1)}), bf16[128,128]{1,0:T(8,128)(2,1)}) %reduce-scatter.76.cloned.1.call-update) | async-done | bytes 32784
  1428.6 22.3 %reduce-scatter.70.cloned.1.call-done = bf16[1,128,3,128]{3,1,2,0:T(8,128)(2,1)} async-done(((bf16[1,512,3,128]{3,1,2,0:T(8,128)(2,1)}), bf16[1,128,3,128]{3,1,2,0:T(8,128)(2,1)}) %reduce-scatter.70.cloned.1.call-update) | async-done | bytes 98320 | tf_op jit(solution)/shard_map/reduce_scatter | solution.py:422
  1452.4 27.8 %reduce-scatter.68.cloned.1.call-done = bf16[256,512]{1,0:T(8,128)(2,1)} async-done(((bf16[1024,512]{1,0:T(8,128)(2,1)}), bf16[256,512]{1,0:T(8,128)(2,1)}) %reduce-scatter.68.cloned.1.call-update) | async-done | bytes 262160 | tf_op jit(solution)/shard_map/reduce_scatter | solution.py:66
  1480.3 28.0 %reduce-scatter.66.cloned.1.call-done = bf16[256,512]{1,0:T(8,128)(2,1)} async-done(((bf16[1024,512]{1,0:T(8,128)(2,1)}), bf16[256,512]{1,0:T(8,128)(2,1)}) %reduce-scatter.66.cloned.1.call-update) | async-done | bytes 262160 | tf_op jit(solution)/shard_map/reduce_scatter | solution.py:66
  1509.7 26.8 %reduce-scatter.74.cloned.1.call-done = bf16[256,512]{1,0:T(8,128)(2,1)} async-done(((bf16[1024,512]{1,0:T(8,128)(2,1)}), bf16[256,512]{1,0:T(8,128)(2,1)}) %reduce-scatter.74.cloned.1.call-update) | async-done | bytes 262160 | tf_op jit(solution)/shard_map/reduce_scatter | solution.py:66
  1543.3 48.9 %reduce-scatter.82.cloned.1.call-done = f32[32,3]{1,0:T(8,128)} async-done(((f32[512,3]{1,0:T(8,128)}), f32[32,3]{1,0:T(8,128)}) %reduce-scatter.82.cloned.1.call-update) | async-done | bytes 400
  1593.9 56.2 %reduce-scatter.80.cloned.1.call-done = f32[32,3]{1,0:T(8,128)} async-done(((f32[512,3]{1,0:T(8,128)}), f32[32,3]{1,0:T(8,128)}) %reduce-scatter.80.cloned.1.call-update) | async-done | bytes 400
  (1134 shorter events, 450.4 us)
Async XLA Ops:
  7.2 107.3 %all-gather.18.cloned.1.call-start = ((), (), s32[]{:S(2)}) async-start(), calls=%async_computation.25 | async-start | bytes 1310720 | tf_op jit(solution)/shard_map/all_gather | solution.py:62
  47.3 174.4 %copy-start.151 = (f32[512]{0:T(512)}, f32[512]{0:T(512)S(1)}, u32[]{:S(2)}) copy-start(f32[512]{0:T(512)S(1)} %get-tuple-element.1504) | copy-start | bytes 6148
  84.5 69.1 %reduce-scatter.40.cloned.1.call-start = ((), (), s32[]{:S(2)}) async-start(), calls=%async_computation.26 | async-start | bytes 1310720 | tf_op jit(solution)/shard_map/reduce_scatter | solution.py:66
  93.8 229.7 %copy-start.49 = (bf16[1,128,512]{2,1,0:T(8,128)(2,1)}, bf16[1,128,512]{2,1,0:T(8,128)(2,1)S(1)}, u32[]{:S(2)}) copy-start(bf16[1,128,512]{2,1,0:T(8,128)(2,1)S(1)} %all_gather.83) | copy-start | bytes 393220
  126.9 57.9 %all-gather.20.cloned.1.call-start = ((), (), s32[]{:S(2)}) async-start(), calls=%async_computation.27 | async-start | bytes 1310720 | tf_op jit(solution)/shard_map/all_gather | solution.py:62
  157.9 63.7 %reduce-scatter.42.cloned.1.call-start = ((), (), s32[]{:S(2)}) async-start(), calls=%async_computation.28 | async-start | bytes 1310720 | tf_op jit(solution)/shard_map/reduce_scatter | solution.py:66
  165.8 401.2 %copy-start.116 = (bf16[1,512,512]{2,1,0:T(8,128)(2,1)}, bf16[1,512,512]{2,1,0:T(8,128)(2,1)S(1)}, u32[]{:S(2)}) copy-start(bf16[1,512,512]{2,1,0:T(8,128)(2,1)S(1)} %all_gather.85) | copy-start | bytes 1572868
  173.1 229.5 %copy-start.120 = (bf16[1,512,512]{2,1,0:T(8,128)(2,1)}, bf16[1,512,512]{2,1,0:T(8,128)(2,1)S(1)}, u32[]{:S(2)}) copy-start(bf16[1,512,512]{2,1,0:T(8,128)(2,1)S(1)} %all_gather.86) | copy-start | bytes 1572868
  194.9 58.0 %all-gather.22.cloned.1.call-start = ((), (), s32[]{:S(2)}) async-start(), calls=%async_computation.29 | async-start | bytes 1310720 | tf_op jit(solution)/shard_map/all_gather | solution.py:62
  223.6 74.4 %all-gather.24.cloned.1.call-start = ((), (), s32[]{:S(2)}) async-start(), calls=%async_computation.31 | async-start | bytes 2621440 | tf_op jit(solution)/shard_map/all_gather | solution.py:62
  224.1 7.0 collective-permute-start
  232.3 105.2 %reduce-scatter.46.cloned.1.call-start = ((), (), s32[]{:S(2)}) async-start(), calls=%async_computation.32 | async-start | bytes 1310720 | tf_op jit(solution)/shard_map/reduce_scatter | solution.py:66
  241.6 440.2 %copy-start.94 = (bf16[512,64]{0,1:T(8,128)(2,1)}, bf16[512,64]{0,1:T(8,128)(2,1)S(1)}, u32[]{:S(2)}) copy-start(bf16[512,64]{0,1:T(8,128)(2,1)S(1)} %all_gather.89) | copy-start | bytes 196612
  246.9 385.3 %copy-start.68 = (bf16[64,512]{1,0:T(8,128)(2,1)}, bf16[64,512]{1,0:T(8,128)(2,1)S(1)}, u32[]{:S(2)}) copy-start(bf16[64,512]{1,0:T(8,128)(2,1)S(1)} %all_gather.91) | copy-start | bytes 196612
  252.9 426.3 %copy-start.80 = (bf16[512,2,64]{0,2,1:T(8,128)(2,1)}, bf16[512,2,64]{0,2,1:T(8,128)(2,1)S(1)}, u32[]{:S(2)}) copy-start(bf16[512,2,64]{0,2,1:T(8,128)(2,1)S(1)} %all_gather.90) | copy-start | bytes 393220
  311.6 54.1 %reduce-scatter.44.cloned.1.call-start = ((), (), s32[]{:S(2)}) async-start(), calls=%async_computation.30 | async-start | bytes 1310720 | tf_op jit(solution)/shard_map/reduce_scatter | solution.py:66
  324.9 70.2 %all-gather.26.cloned.1.call-start = ((), (), s32[]{:S(2)}) async-start(), calls=%async_computation.33 | async-start | bytes 1310720 | tf_op jit(solution)/shard_map/all_gather | solution.py:62
  337.5 28.2 %collective-permute-start.1 = (bf16[256,512]{1,0:T(8,128)(2,1)}, bf16[256,512]{1,0:T(8,128)(2,1)}, u32[]{:S(2)}, u32[]{:S(2)}) collective-permute-start(bf16[256,512]{1,0:T(8,128)(2,1)} %reduce-scatter.46.cloned.1.call-done), channel_id=1, source_target_pairs={{0,16},{1,17},{2,18},{3,19},{4,20},{5,21},{6,22},{7,23},{8,24},{9,... | collective-permute-start | bytes 786440 | tf_op jit(solution)/shard_map/ppermute | solution.py:29
  368.3 63.8 %reduce-scatter.48.cloned.1.call-start = ((), (), s32[]{:S(2)}) async-start(), calls=%async_computation.34 | async-start | bytes 1310720 | tf_op jit(solution)/shard_map/reduce_scatter | solution.py:66
  405.4 82.5 %all-gather.28.cloned.1.call-start = ((), (), s32[]{:S(2)}) async-start(), calls=%async_computation.35 | async-start | bytes 2621440 | tf_op jit(solution)/shard_map/all_gather | solution.py:62
  433.7 7.1 collective-permute-start.2
  441.9 85.8 %reduce-scatter.50.cloned.1.call-start = ((), (), s32[]{:S(2)}) async-start(), calls=%async_computation.36 | async-start | bytes 1310720 | tf_op jit(solution)/shard_map/reduce_scatter | solution.py:66
  501.9 65.1 %all-gather.30.cloned.1.call-start = ((), (), s32[]{:S(2)}) async-start(), calls=%async_computation.37 | async-start | bytes 1310720 | tf_op jit(solution)/shard_map/all_gather | solution.py:62
  527.7 9.1 collective-permute-start.3
  539.2 64.8 %reduce-scatter.52.cloned.1.call-start = ((), (), s32[]{:S(2)}) async-start(), calls=%async_computation.38 | async-start | bytes 1310720 | tf_op jit(solution)/shard_map/reduce_scatter | solution.py:66
  577.2 54.9 %all-gather.34.cloned.1.call-start = ((), (), s32[]{:S(2)}) async-start(), calls=%async_computation.40 | async-start | bytes 1310720 | tf_op jit(solution)/shard_map/all_gather | solution.py:62
  577.3 7.0 collective-permute-start.5
  585.1 94.2 %all-gather.32.cloned.1.call-start = ((), (), s32[]{:S(2)}) async-start(), calls=%async_computation.39 | async-start | bytes 2621440 | tf_op jit(solution)/shard_map/all_gather | solution.py:62
  605.6 7.0 collective-permute-start.4
  613.7 140.0 %reduce-scatter.54.cloned.1.call-start = ((), (), s32[]{:S(2)}) async-start(), calls=%async_computation.41 | async-start | bytes 2621440 | tf_op jit(solution)/shard_map/reduce_scatter | solution.py:66
  711.1 81.5 %all-gather.36.cloned.1.call-start = ((), (), s32[]{:S(2)}) async-start(), calls=%async_computation.42 | async-start | bytes 1310720 | tf_op jit(solution)/shard_map/all_gather | solution.py:62
  755.0 7.0 collective-permute-start.6
  764.1 62.0 %reduce-scatter.56.cloned.1.call-start = ((), (), s32[]{:S(2)}) async-start(), calls=%async_computation.43 | async-start | bytes 1310720 | tf_op jit(solution)/shard_map/reduce_scatter | solution.py:66
  799.3 69.3 %all-gather.38.cloned.1.call-start = ((), (), s32[]{:S(2)}) async-start(), calls=%async_computation.44 | async-start | bytes 1310720 | tf_op jit(solution)/shard_map/all_gather | solution.py:62
  832.0 7.0 collective-permute-start.7
  839.8 98.3 %reduce-scatter.58.cloned.1.call-start = ((), (), s32[]{:S(2)}) async-start(), calls=%async_computation.45 | async-start | bytes 2621440 | tf_op jit(solution)/shard_map/reduce_scatter | solution.py:66
  894.6 82.4 %all-gather.40.cloned.1.call-start = ((), (), s32[]{:S(2)}) async-start(), calls=%async_computation.46 | async-start | bytes 1310720 | tf_op jit(solution)/shard_map/all_gather | solution.py:62
  939.3 7.0 collective-permute-start.8
  948.3 62.1 %reduce-scatter.60.cloned.1.call-start = ((), (), s32[]{:S(2)}) async-start(), calls=%async_computation.47 | async-start | bytes 1310720 | tf_op jit(solution)/shard_map/reduce_scatter | solution.py:66
  983.6 69.5 %all-gather.42.cloned.1.call-start = ((), (), s32[]{:S(2)}) async-start(), calls=%async_computation.48 | async-start | bytes 1310720 | tf_op jit(solution)/shard_map/all_gather | solution.py:62
  1016.4 7.1 collective-permute-start.9
  1024.2 99.8 %reduce-scatter.62.cloned.1.call-start = ((), (), s32[]{:S(2)}) async-start(), calls=%async_computation.49 | async-start | bytes 2621440 | tf_op jit(solution)/shard_map/reduce_scatter | solution.py:66
  1080.6 82.4 %all-gather.44.cloned.1.call-start = ((), (), s32[]{:S(2)}) async-start(), calls=%async_computation.50 | async-start | bytes 1310720 | tf_op jit(solution)/shard_map/all_gather | solution.py:62
  1125.3 7.0 collective-permute-start.10
  1134.4 58.0 %all-gather.50.cloned.1.call-start = ((), (), s32[]{:S(2)}) async-start(), calls=%async_computation.56 | async-start | bytes 1310720 | tf_op jit(solution)/shard_map/all_gather | solution.py:62
  1134.9 86.4 %reduce-scatter.64.cloned.1.call-start = ((), (), s32[]{:S(2)}) async-start(), calls=%async_computation.51 | async-start | bytes 1310720 | tf_op jit(solution)/shard_map/reduce_scatter | solution.py:66
  1169.6 116.5 %all-gather.48.cloned.1.call-start = ((), (), s32[]{:S(2)}) async-start(), calls=%async_computation.54 | async-start | bytes 1310720 | tf_op jit(solution)/shard_map/all_gather | solution.py:62
  1228.1 91.8 %all-gather.46.cloned.1.call-start = ((), (), s32[]{:S(2)}) async-start(), calls=%async_computation.52 | async-start | bytes 1310720 | tf_op jit(solution)/shard_map/all_gather | solution.py:62
  1263.8 110.1 %reduce-scatter.88.cloned.1.call-start = ((), (), s32[]{:S(2)}) async-start(), calls=%async_computation.66 | async-start | bytes 163840
  1270.9 104.5 %reduce-scatter.84.cloned.1.call-start = ((), (), s32[]{:S(2)}) async-start(), calls=%async_computation.64 | async-start | bytes 163840
  1273.3 103.6 %reduce-scatter.86.cloned.1.call-start = ((), (), s32[]{:S(2)}) async-start(), calls=%async_computation.65 | async-start | bytes 163840
  1275.9 104.7 %reduce-scatter.78.cloned.1.call-start = ((), (), s32[]{:S(2)}) async-start(), calls=%async_computation.61 | async-start | bytes 655360
  1280.2 124.8 %reduce-scatter.72.cloned.1.call-start = ((), (), s32[]{:S(2)}) async-start(), calls=%async_computation.58 | async-start | bytes 655360 | tf_op jit(solution)/shard_map/reduce_scatter | solution.py:431
  1286.1 140.9 %reduce-scatter.76.cloned.1.call-start = ((), (), s32[]{:S(2)}) async-start(), calls=%async_computation.60 | async-start | bytes 163840
  1362.7 88.2 %reduce-scatter.70.cloned.1.call-start = ((), (), s32[]{:S(2)}) async-start(), calls=%async_computation.57 | async-start | bytes 491520 | tf_op jit(solution)/shard_map/reduce_scatter | solution.py:422
  1367.3 112.9 %reduce-scatter.68.cloned.1.call-start = ((), (), s32[]{:S(2)}) async-start(), calls=%async_computation.55 | async-start | bytes 1310720 | tf_op jit(solution)/shard_map/reduce_scatter | solution.py:66
  1369.2 139.0 %reduce-scatter.66.cloned.1.call-start = ((), (), s32[]{:S(2)}) async-start(), calls=%async_computation.53 | async-start | bytes 1310720 | tf_op jit(solution)/shard_map/reduce_scatter | solution.py:66
  1371.0 165.5 %reduce-scatter.74.cloned.1.call-start = ((), (), s32[]{:S(2)}) async-start(), calls=%async_computation.59 | async-start | bytes 1310720 | tf_op jit(solution)/shard_map/reduce_scatter | solution.py:66
  1372.8 219.4 %reduce-scatter.82.cloned.1.call-start = ((), (), s32[]{:S(2)}) async-start(), calls=%async_computation.63 | async-start | bytes 278528
  1373.1 163.4 %copy-start.198 = (f32[256]{0:T(256)S(1)}, f32[256]{0:T(256)}, u32[]{:S(2)}) copy-start(f32[256]{0:T(256)} %copy-done.197) | copy-start | bytes 3076
  1373.1 163.4 %copy-start.200 = (f32[256]{0:T(256)S(1)}, f32[256]{0:T(256)}, u32[]{:S(2)}) copy-start(f32[256]{0:T(256)} %copy-done.199) | copy-start | bytes 3076
  1382.7 157.3 %copy-start.225 = (f32[512]{0:T(512)S(1)}, f32[512]{0:T(512)}, u32[]{:S(2)}) copy-start(f32[512]{0:T(512)} %get-tuple-element.1467) | copy-start | bytes 6148
  1382.7 157.4 %copy-start.219 = (f32[512]{0:T(512)S(1)}, f32[512]{0:T(512)}, u32[]{:S(2)}) copy-start(f32[512]{0:T(512)} %get-tuple-element.1465) | copy-start | bytes 6148
  1539.7 110.4 %reduce-scatter.80.cloned.1.call-start = ((), (), s32[]{:S(2)}) async-start(), calls=%async_computation.62 | async-start | bytes 278528
  (258 other events, 6674.4 us)
Sparse Core Ops, SparseCore 0:
  84.6 29.8 all-gather.17
  127.0 26.6 reduce-scatter.39
  158.1 26.6 all-gather.19
  195.0 26.5 reduce-scatter.41
  223.7 26.6 all-gather.21
  252.4 45.5 all-gather.23
  311.8 25.7 reduce-scatter.45
  339.9 25.7 reduce-scatter.43
  368.5 26.6 all-gather.25
  405.5 26.5 reduce-scatter.47
  442.0 45.8 all-gather.27
  502.0 25.6 reduce-scatter.49
  539.3 27.6 all-gather.29
  577.3 26.6 reduce-scatter.51
  605.5 26.6 all-gather.33
  633.6 45.5 all-gather.31
  711.3 42.4 reduce-scatter.53
  764.2 28.3 all-gather.35
  799.4 26.6 reduce-scatter.55
  839.9 28.7 all-gather.37
  894.7 43.3 reduce-scatter.57
  948.5 28.4 all-gather.39
  983.8 26.6 reduce-scatter.59
  1024.3 28.7 all-gather.41
  1080.7 43.3 reduce-scatter.61
  1134.5 28.4 all-gather.43
  1164.9 27.4 all-gather.49
  1194.7 26.6 reduce-scatter.63
  1228.2 26.5 all-gather.47
  1263.9 26.7 all-gather.45
  1293.3 18.4 reduce-scatter.87
  1314.3 19.6 reduce-scatter.83
  1336.4 19.5 reduce-scatter.85
  1358.5 22.1 reduce-scatter.77
  1383.3 21.6 reduce-scatter.71
  1407.9 19.1 reduce-scatter.75
  1429.5 21.2 reduce-scatter.69
  1453.2 26.9 reduce-scatter.67
  1482.4 25.7 reduce-scatter.65
  1510.6 25.7 reduce-scatter.73
  1540.0 52.2 reduce-scatter.81
  1595.8 54.3 reduce-scatter.79
where the time goes:
time: 1670 us; the launch traced here: 1660 us
  waiting for transfers between devices  1080 us (65%)
  matrix products  259 us (16%)
  blocking collectives  111 us (7%)
  other arithmetic  101 us (6%)
  local copies, waits for them, and re-layouts  75.7 us (5%)
  between operations  18.2 us (1%)
    reduce_scatter x16, waiting for transfers between devices, scatter_rows(): lax.psum_scatter(term_fn(jnp.int32(0), local_rows * lax.axis_size('mp'))....  457 us
    all_gather x17, waiting for transfers between devices, gather_rows(): return lax.all_gather(row_piece, 'mp', axis=0, tiled=True)  386 us
    unnamed x49, waiting for transfers between devices  129 us
    dot_general x60, matrix products, product(): return jnp.dot(left_side, right_side, preferred_element_type=jnp.float32)  114 us
    ppermute x6, waiting for transfers between devices, from_partner(): return lax.ppermute(block, axis, route)  40.1 us
    dot_general x22, matrix products, masked_scores(): jnp.einsum('qhe,khe->hqk', queries, key_rows, preferred_element_type=jnp....  38.5 us
  transfers between devices with their start and end apart: 53, of which 46 were waited for; matrix products, arithmetic and copies ran while one was open for 12% of the time, Pallas kernels for 0%

commit v1 on v0

v1 whole, which is shorter than its diff:
```python
import jax
import jax.numpy as jnp
from jax import lax
from jax.sharding import PartitionSpec as P

HD = 64
EPS = 1e-05
NEG = -1e30
BF = jnp.bfloat16
F32 = jnp.float32


def swap(block, axis, bit):
    count = lax.axis_size(axis)
    return lax.ppermute(block, axis, [(i, i ^ bit) for i in range(count)])


def oneway(block, axis, source, target):
    return lax.ppermute(block, axis, [(source, target)])


def dp_bits():
    count = lax.axis_size("dp")
    return [1 << b for b in range(1, count.bit_length() - 1)]


def gather_blocks(shard):
    ways = lax.axis_size("mp")
    tiled = jnp.broadcast_to(shard[None], (ways,) + shard.shape)
    blocks = [(0, lax.all_to_all(tiled, "mp", 0, 0, tiled=True))]
    for bit in dp_bits():
        blocks = blocks + [(a ^ bit, swap(b, "dp", bit)) for a, b in blocks]
    return blocks + [(a ^ 1, swap(b, "dp", 1)) for a, b in blocks]


def relative_order():
    order = [0]
    for bit in dp_bits():
        order = order + [a ^ bit for a in order]
    return order + [a ^ 1 for a in order]


def assemble(blocks):
    order = {a: b for a, b in blocks}
    stacked = jnp.stack([order[a] for a in range(len(blocks))])
    me = lax.axis_index("dp")
    stacked = jnp.take(stacked, jnp.arange(len(blocks)) ^ me, axis=0)
    count, ways, blk, cols = stacked.shape
    return stacked.transpose(1, 0, 2, 3).reshape(ways, count * blk, cols)


def to_relative(grad):
    count = lax.axis_size("dp")
    ways, depth, cols = grad.shape
    me = lax.axis_index("dp")
    tiles = grad.astype(BF).reshape(ways, count, depth // count, cols).transpose(1, 0, 2, 3)
    return jnp.take(tiles, jnp.array(relative_order()) ^ me, axis=0)


def reduce_blocks(grad):
    for bit in [1] + dp_bits()[::-1]:
        half = grad.shape[0] // 2
        other = swap(grad[half:], "dp", bit)
        grad = (grad[:half].astype(F32) + other.astype(F32)).astype(BF)
    parts = lax.all_to_all(grad[0], "mp", 0, 0, tiled=True)
    return jnp.sum(parts.astype(F32), axis=0)


def rows_in(local, core):
    rows, span, width = local.shape
    halves = local.reshape(rows, 2, span // 2, width)
    first = core == 0
    keep = jnp.where(first, halves[:, 0], halves[:, 1])
    send = jnp.where(first, halves[:, 1], halves[:, 0])
    other = swap(send, "dp", 1)
    chip = jnp.where(first, jnp.concatenate([keep, other]), jnp.concatenate([other, keep]))
    return lax.all_to_all(chip, "mp", 0, 0, tiled=True).reshape(-1, width)


def rows_out(own, core, rows):
    width = own.shape[-1]
    ways = lax.axis_size("mp")
    chip = lax.all_to_all(own.reshape(ways, -1, width), "mp", 0, 0, tiled=True)
    first = core == 0
    keep = jnp.where(first, chip[:rows], chip[rows:])
    send = jnp.where(first, chip[rows:], chip[:rows])
    other = swap(send, "dp", 1)
    low = jnp.where(first, keep, other)
    high = jnp.where(first, other, keep)
    return jnp.concatenate([low, high], axis=1)


def stats(states):
    average = jnp.mean(states, axis=-1, keepdims=True)
    centred = states - average
    inv = lax.rsqrt(jnp.mean(centred * centred, axis=-1, keepdims=True) + EPS)
    return centred * inv, inv


def norm_fwd(states, gain, bias):
    hat, _ = stats(states)
    return (hat * gain + bias).astype(BF)


def norm_bwd(states, gain, grad):
    hat, inv = stats(states)
    e = grad * gain
    dx = inv * (
        e - jnp.mean(e, axis=-1, keepdims=True) - hat * jnp.mean(e * hat, axis=-1, keepdims=True)
    )
    return dx, jnp.sum(grad * hat, axis=0), jnp.sum(grad, axis=0)


def mm(a, b):
    return jnp.dot(a, b, preferred_element_type=F32)


def nt(a, b):
    return lax.dot_general(a, b, (((1,), (1,)), ((), ())), preferred_element_type=F32)


def tn(a, b):
    return lax.dot_general(a, b, (((0,), (0,)), ((), ())), preferred_element_type=F32)


def heads(x):
    return x.reshape(x.shape[0], -1, HD)


def attn_fwd(q, k, v, seg_q, seg_k):
    s = jnp.einsum("qhe,khe->hqk", heads(q), heads(k), preferred_element_type=F32) * HD**-0.5
    s = jnp.where((seg_q[:, None] == seg_k[None, :])[None], s, NEG)
    top = jnp.max(s, axis=-1, keepdims=True)
    w = jnp.exp(s - top)
    total = jnp.sum(w, axis=-1, keepdims=True)
    p = (w / total).astype(BF)
    o = jnp.einsum("hqk,khe->qhe", p, heads(v), preferred_element_type=F32)
    return o.astype(BF).reshape(q.shape), (top + jnp.log(total))[..., 0]


def attn_bwd(q, k, v, seg_q, seg_k, lse, do):
    s = jnp.einsum("qhe,khe->hqk", heads(q), heads(k), preferred_element_type=F32) * HD**-0.5
    s = jnp.where((seg_q[:, None] == seg_k[None, :])[None], s, NEG)
    p = jnp.exp(s - lse[..., None])
    dp = jnp.einsum("qhe,khe->hqk", heads(do), heads(v), preferred_element_type=F32)
    ds = (p * (dp - jnp.sum(p * dp, axis=-1, keepdims=True))).astype(BF)
    dq = jnp.einsum("hqk,khe->qhe", ds, heads(k), preferred_element_type=F32) * HD**-0.5
    dk = jnp.einsum("hqk,qhe->khe", ds, heads(q), preferred_element_type=F32) * HD**-0.5
    dv = jnp.einsum("hqk,qhe->khe", p.astype(BF), heads(do), preferred_element_type=F32)
    return (
        dq.astype(BF).reshape(q.shape),
        dk.astype(BF).reshape(k.shape),
        dv.astype(BF).reshape(k.shape),
    )


def cols(weight, at):
    ways, depth, _ = weight.shape
    return weight[:, :, at * 128 : at * 128 + 128].transpose(1, 0, 2).reshape(depth, ways * 128)


def pack(parts, ways):
    depth = parts[0].shape[0]
    return jnp.concatenate(
        [p.reshape(depth, ways, -1).transpose(1, 0, 2) for p in parts], axis=-1
    )


def self_fwd(x_full, seg, w1, gain, bias):
    own = x_full.shape[0] // 2
    normed = norm_fwd(x_full.astype(F32), gain, bias)
    q = mm(normed[:own], cols(w1, 0)).astype(BF)
    k = mm(normed, cols(w1, 1)).astype(BF)
    v = mm(normed, cols(w1, 2)).astype(BF)
    att, lse = attn_fwd(q, k, v, seg[:own], seg)
    mid = x_full[:own].astype(F32) + nt(att, cols(w1, 3))
    return normed, q, k, v, att, lse, mid


def self_bwd(d_mid, normed, q, k, v, att, lse, seg, w1):
    own = q.shape[0]
    ways = w1.shape[0]
    low = d_mid.astype(BF)
    d_out = tn(low, att)
    d_att = mm(low, cols(w1, 3)).astype(BF)
    dq, dk, dv = attn_bwd(q, k, v, seg[:own], seg, lse, d_att)
    grads = pack([tn(normed[:own], dq), tn(normed, dk), tn(normed, dv), d_out], ways)
    d_normed = nt(dk, cols(w1, 1)) + nt(dv, cols(w1, 2))
    return nt(dq, cols(w1, 0)) + d_normed[:own], d_normed[own:].astype(BF), grads


def up_down(w2):
    ways, depth, both = w2.shape
    half = both // 2
    up = w2[:, :, :half].transpose(1, 0, 2).reshape(depth, ways * half)
    down = w2[:, :, half:].transpose(1, 0, 2).reshape(depth, ways * half)
    return up, down


def feed_fwd(states, w2, gain, bias):
    up, down = up_down(w2)
    normed = norm_fwd(states, gain, bias)
    pre = mm(normed, up)
    cdf = 0.5 * (1.0 + lax.erf(pre * 0.5**0.5))
    hidden = (pre * cdf).astype(BF)
    slope = (cdf + pre * jnp.exp(-0.5 * pre * pre) * 0.3989422804014327).astype(BF)
    return states + nt(hidden, down), hidden, slope


def feed_bwd(states, cot, hidden, slope, w2, gain, bias):
    up, down = up_down(w2)
    normed = norm_fwd(states, gain, bias)
    low = cot.astype(BF)
    d_down = tn(low, hidden)
    d_pre = (mm(low, down) * slope.astype(F32)).astype(BF)
    d_up = tn(normed, d_pre)
    dx, d_gain, d_bias = norm_bwd(states, gain, nt(d_pre, up))
    return cot + dx, pack([d_up, d_down], w2.shape[0]), d_gain, d_bias


def cross_both(mid, mem, cot, seg_q, seg_k, w2, w3, gains, biases):
    ways = w3.shape[0]
    cross_in = norm_fwd(mid, gains[2], biases[2])
    q = mm(cross_in, cols(w3, 0)).astype(BF)
    k = mm(mem, cols(w3, 1)).astype(BF)
    v = mm(mem, cols(w3, 2)).astype(BF)
    att, lse = attn_fwd(q, k, v, seg_q, seg_k)
    joined = mid + nt(att, cols(w3, 3))
    decoded, hidden, slope = feed_fwd(joined, w2, gains[1], biases[1])
    d_joined, grad2, dg1, db1 = feed_bwd(joined, cot, hidden, slope, w2, gains[1], biases[1])
    low = d_joined.astype(BF)
    d_oc = tn(low, att)
    d_att = mm(low, cols(w3, 3)).astype(BF)
    dq, dk, dv = attn_bwd(q, k, v, seg_q, seg_k, lse, d_att)
    grad3 = pack([tn(cross_in, dq), tn(mem, dk), tn(mem, dv), d_oc], ways)
    d_mem = (nt(dk, cols(w3, 1)) + nt(dv, cols(w3, 2))).astype(BF)
    dx, dg2, db2 = norm_bwd(mid, gains[2], nt(dq, cols(w3, 0)))
    small = jnp.stack([dg1, dg2, db1, db2])
    return decoded.astype(BF), d_joined + dx, d_mem, grad2, grad3, small


def on_device(layer_in, segment_ids, out_grads, w_qkv, w_out, w_up, w_down, norm_gain, norm_bias, w_qc, w_kvc, w_oc):
    encoder = lax.axis_index("section") == 0
    core = lax.axis_index("dp") & 1
    place = lax.axis_index("mp")
    ways = lax.axis_size("mp")
    rows = layer_in.shape[1]
    width = layer_in.shape[3]
    blk = w_qkv.shape[1]

    shard1 = jnp.concatenate([w_qkv[0].reshape(blk, -1), w_out[0].T], axis=1)
    shard2 = jnp.concatenate([w_up[0], w_down[0].T], axis=1)
    mine3 = jnp.stack([w_qc, w_kvc[:, 0], w_kvc[:, 1], w_oc.T], axis=1)
    theirs3 = swap(mine3, "section", 1)
    shard3 = jnp.where(
        encoder,
        jnp.concatenate([mine3, theirs3], axis=2),
        jnp.concatenate([theirs3, mine3], axis=2),
    ).reshape(blk, -1)
    own = rows_in(layer_in[0], core)
    w1 = assemble(gather_blocks(shard1))
    norms = jnp.concatenate([norm_gain[0], norm_bias[0]])
    norms = lax.all_gather(norms, ("dp", "mp"), axis=1, tiled=True)
    gains, biases = norms[:3], norms[3:]
    w2 = assemble(gather_blocks(shard2))
    w3 = assemble(gather_blocks(shard3))
    cots = rows_in(out_grads[0], core).astype(F32)

    other_segs = swap(segment_ids, "dp", 1)
    segs = jnp.where(
        core == 0,
        jnp.concatenate([segment_ids, other_segs], axis=1),
        jnp.concatenate([other_segs, segment_ids], axis=1),
    )
    segs = lax.dynamic_index_in_dim(segs, place, axis=1, keepdims=False)
    segs = segs.reshape(2, ways, 2, -1)
    even, odd = segs[:, :, 0].reshape(2, -1), segs[:, :, 1].reshape(2, -1)
    segs = jnp.where(
        core == 0, jnp.concatenate([even, odd], axis=1), jnp.concatenate([odd, even], axis=1)
    )
    half = segs.shape[1] // 2
    seg_own = jnp.where(encoder, segs[0], segs[1])

    x_full = jnp.concatenate([own, swap(own, "dp", 1)])
    normed, q, k, v, att, lse, mid = self_fwd(x_full, seg_own, w1, gains[0], biases[0])

    def encode(_):
        out, hidden, slope = feed_fwd(mid, w2, gains[1], biases[1])
        return out, norm_fwd(out, gains[2], biases[2]), hidden, slope

    wide = (half, shard2.shape[1] // 2 * ways)

    def skip(_):
        return (
            jnp.zeros((half, width), F32),
            jnp.zeros((half, width), BF),
            jnp.zeros(wide, BF),
            jnp.zeros(wide, BF),
        )

    encoded, memory, hidden, slope = lax.cond(encoder, encode, skip, 0)
    mem_own = oneway(memory, "section", 0, 1)
    mem_full = jnp.concatenate([mem_own, swap(mem_own, "dp", 1)])

    def decode(_):
        return cross_both(mid, mem_full, cots, segs[1, :half], segs[0], w2, w3, gains, biases)

    def skip2(_):
        return jax.tree.map(
            lambda s: jnp.zeros(s.shape, s.dtype), jax.eval_shape(decode, 0)
        )

    decoded, d_mid, d_mem, grad2, grad3, small = lax.cond(encoder, skip2, decode, 0)
    section_out = rows_out(jnp.where(encoder, memory, decoded), core, rows)[None]
    d_mem = (d_mem[:half].astype(F32) + swap(d_mem[half:], "dp", 1).astype(F32)).astype(BF)
    d_mem = oneway(d_mem, "section", 1, 0)

    def encode_back(_):
        d_out, dg2, db2 = norm_bwd(encoded, gains[2], d_mem.astype(F32) + cots)
        d, g2, dg1, db1 = feed_bwd(mid, d_out, hidden, slope, w2, gains[1], biases[1])
        return d, g2, jnp.stack([dg1, dg2, db1, db2])

    d_mid, grad2, small = lax.cond(encoder, encode_back, lambda _: (d_mid, grad2, small), 0)
    d_own, d_other, grad1 = self_bwd(d_mid, normed, q, k, v, att, lse, seg_own, w1)
    d_own = d_own + swap(d_other, "dp", 1).astype(F32)
    dx, dg0, db0 = norm_bwd(own.astype(F32), gains[0], d_own)
    in_grads = rows_out((d_mid + dx).astype(BF), core, rows)[None]

    r2 = reduce_blocks(to_relative(grad2))
    r3 = reduce_blocks(to_relative(grad3))
    r1 = reduce_blocks(to_relative(grad1))
    grad_qkv = r1[:, :384].reshape(1, blk, 3, -1)
    grad_out = r1[:, 384:].T[None]
    span = r2.shape[1] // 2
    grad_up = r2[None, :, :span]
    grad_down = r2[:, span:].T[None]
    r3 = r3.reshape(blk, 4, 2, -1)
    back = oneway(r3[:, :, 0].astype(BF), "section", 1, 0).astype(F32)
    r3 = jnp.where(encoder, back, r3[:, :, 1])
    grad_qc, grad_kvc, grad_oc = r3[:, 0], r3[:, 1:3], r3[:, 3].T
    small = jnp.concatenate([dg0[None], small[:2], db0[None], small[2:]])
    small = lax.psum_scatter(small, ("dp", "mp"), scatter_dimension=1, tiled=True)
    grad_gain = small[None, :3]
    grad_bias = jnp.stack([small[3], small[5]])[None]
    grad_ffn = small[4][None]
    return (
        section_out,
        in_grads,
        grad_qkv,
        grad_out,
        grad_up,
        grad_down,
        grad_gain,
        grad_bias,
        grad_ffn,
        grad_qc,
        grad_kvc,
        grad_oc,
    )


def solution(mesh):
    placed = (
        P("section", "dp", "mp", None),
        P(None, "dp", None),
        P("section", "dp", "mp", None),
        P("section", "dp", None, "mp"),
        P("section", "mp", "dp"),
        P("section", "dp", "mp"),
        P("section", "mp", "dp"),
        P("section", None, ("dp", "mp")),
        P("section", None, ("dp", "mp")),
        P("dp", ("section", "mp")),
        P("dp", None, ("section", "mp")),
        P(("section", "mp"), "dp"),
    )
    return jax.shard_map(
        on_device,
        mesh=mesh,
        in_specs=placed,
        out_specs=(
            P("section", "dp", "mp", None),
            P("section", "dp", "mp", None),
            P("section", "dp", None, "mp"),
            P("section", "mp", "dp"),
            P("section", "dp", "mp"),
            P("section", "mp", "dp"),
            P("section", None, ("dp", "mp")),
            P("section", None, ("dp", "mp")),
            P("section", ("dp", "mp")),
            P("dp", ("section", "mp")),
            P("dp", None, ("section", "mp")),
            P(("section", "mp"), "dp"),
        ),
        check_vma=False,
    )
```

time: 1670 us -> 649 us (0.39)
  waiting for transfers between devices: 1080 us -> 159 us
  matrix products: 259 us -> 116 us
  blocking collectives: 111 us -> 33.9 us
  starting transfers between devices: 14.3 us -> 77.1 us
  local copies, waits for them, and re-layouts: 75.7 us -> 123 us
    reduce_scatter x18 -> x0, waiting for transfers between devices: 502 us -> none  [the longest x16 457 us: scatter_rows(): lax.psum_scatter(term_fn(jnp.int32(0), local_rows * lax.axis_size('mp'))....]
    all_gather x17 -> x0, waiting for transfers between devices: 386 us -> none  [gather_rows(): return lax.all_gather(row_piece, 'mp', axis=0, tiled=True)]
    dot_general x140 -> x42, matrix products: 259 us -> 116 us  [the longest x2 23.9 us: attn_bwd(): jnp.einsum('qhe,khe->hqk', heads(do), heads(v), preferred_element_type=F32)]
    all_gather x9 -> x1, blocking collectives: 111 us -> 33.9 us  [on_device(): norms = lax.all_gather(norms, ('dp', 'mp'), axis=1, tiled=True)]
    unnamed x49 -> x2, waiting for transfers between devices: 129 us -> 71.2 us
    all_to_all x0 -> x10, waiting for transfers between devices: none -> 46.1 us  [the longest x3 20.3 us: reduce_blocks(): parts = lax.all_to_all(grad[0], 'mp', 0, 0, tiled=True)]
    all_to_all x0 -> x10, starting transfers between devices: none -> 43.5 us  [the longest x3 13.5 us: gather_blocks(): blocks = [(0, lax.all_to_all(tiled, 'mp', 0, 0, tiled=True))]]
    gather x0 -> x6, local copies, waits for them, and re-layouts: none -> 25 us  [the longest x3 12.7 us: to_relative(): return jnp.take(tiles, jnp.array(relative_order()) ^ me, axis=0)]
  transfers between devices with their start and end apart: 53 -> 39, of which waited for: 46 -> 11; matrix products, arithmetic and copies ran while one was open for 12% -> 30% of each run, Pallas kernels for 0% -> 0%
where the time goes in v1:
time: 649 us; the launch traced here: 641 us
  waiting for transfers between devices  159 us (24%)
  local copies, waits for them, and re-layouts  123 us (19%)
  matrix products  116 us (18%)
  other arithmetic  104 us (16%)
  starting transfers between devices  77.1 us (12%)
  blocking collectives  33.9 us (5%)
  between operations  15.5 us (2%)
  loops' own time  12.8 us (2%)
    unnamed x2, waiting for transfers between devices  71.2 us
    all_gather x1, blocking collectives, on_device(): norms = lax.all_gather(norms, ('dp', 'mp'), axis=1, tiled=True)  33.9 us
    ppermute x3, waiting for transfers between devices, oneway(): return lax.ppermute(block, axis, [(source, target)])  33.4 us
    ppermute x25, starting transfers between devices, swap(): return lax.ppermute(block, axis, [(i, i ^ bit) for i in range(count)])  28.9 us
    dot_general x2, matrix products, attn_bwd(): jnp.einsum('qhe,khe->hqk', heads(do), heads(v), preferred_element_type=F32)  23.9 us
    convert_element_type x2, other arithmetic, attn_bwd(): ds = (p * (dp - jnp.sum(p * dp, axis=-1, keepdims=True))).astype(BF)  20.5 us
    all_to_all x3, waiting for transfers between devices, reduce_blocks(): parts = lax.all_to_all(grad[0], 'mp', 0, 0, tiled=True)  20.3 us
    another operation x9, local copies, waits for them, and re-layouts  19.4 us
  transfers between devices with their start and end apart: 39, of which 11 were waited for; matrix products, arithmetic and copies ran while one was open for 30% of the time, Pallas kernels for 0%

profile of v1, /device:TPU:3, one launch (start us, length us, event | category | flops | bytes accessed | tf_op | source)
XLA Modules:
  0.0 640.6 jit_solution(12178272324503234896)
XLA Ops:
  11.6 4.8 all-to-all-start.1
  18.1 33.9 %all-gather = f32[16,32,6]{1,2,0:T(8,128)S(1)} all-gather(f32[1,32,6]{1,2,0:T(8,128)S(1)} %maximum_bitcast_fusion.3), channel_id=1, replica_groups=mesh['section'=2,'dp'=4,'mp'=4] {'dp','mp'}, dimensions={0}, use_global_device_ids=true | all-gather | bytes 13056 | tf_op jit(solution)/shard_map/all_gather | solution.py:263
  53.3 4.0 all-to-all-start.3
  58.3 10.2 %all-to-all-done.3 = bf16[4,128,512]{2,1,0:T(8,128)(2,1)S(1)} async-done(((bf16[4,128,512]{2,1,0:T(8,128)(2,1)}), bf16[4,128,512]{2,1,0:T(8,128)(2,1)S(1)}, u32[]{:S(2)}, u32[]{:S(2)}) %all-to-all-start.3) | async-done | bytes 524320 | tf_op jit(solution)/shard_map/all_to_all | solution.py:30
  68.5 4.6 all-to-all-start
  73.9 10.3 %all-to-all-done = bf16[4,128,512]{2,1,0:T(8,128)(2,1)S(1)} async-done(((bf16[4,128,512]{2,1,0:T(8,128)(2,1)}), bf16[4,128,512]{2,1,0:T(8,128)(2,1)S(1)}, u32[]{:S(2)}, u32[]{:S(2)}) %all-to-all-start) | async-done | bytes 524320 | tf_op jit(solution)/shard_map/all_to_all | solution.py:77
  85.3 4.6 all-to-all-start.2
  91.5 3.8 collective-permute-start.1
  100.3 7.9 %collective-permute-start.4 = (bf16[4,128,512]{2,1,0:T(8,128)(2,1)}, bf16[4,128,512]{2,1,0:T(8,128)(2,1)}, u32[]{:S(2)}, u32[]{:S(2)}) collective-permute-start(bf16[4,128,512]{2,1,0:T(8,128)(2,1)} %collective-permute-done.3), channel_id=1, source_target_pairs={{0,4},{4,0},{8,12},{12,8},{1,5},{5,1},{9,13},{13,9},{2,6},{6,2},{1... | collective-permute-start | bytes 1572872 | tf_op jit(solution)/shard_map/ppermute | solution.py:15
  108.2 3.3 collective-permute-done.11
  111.5 4.2 collective-permute-start.12
  118.0 4.6 all-to-all-start.4
  124.1 3.0 pad_maximum_fusion.7
  127.1 3.6 gather_fusion
  130.7 3.0 pad_maximum_fusion.8
  133.6 3.6 gather_fusion.2
  137.2 4.0 select_bitcast_fusion.1
  150.4 3.3 fusion.108
  154.5 3.5 fusion.45
  160.3 4.5 fusion.61
  166.7 3.6 pad_maximum_fusion.6
  170.3 5.1 gather_fusion.1
  180.6 4.5 conditional.3
  186.6 33.4 %collective-permute-done.13 = bf16[512,512]{1,0:T(8,128)(2,1)S(1)} collective-permute-done((bf16[512,512]{1,0:T(8,128)(2,1)S(1)}, bf16[512,512]{1,0:T(8,128)(2,1)S(1)}, u32[]{:S(2)}, u32[]{:S(2)}) %collective-permute-start.13) | collective-permute-done | bytes 524320 | tf_op jit(solution)/shard_map/ppermute | solution.py:19
  223.8 136.8 %conditional.4 = (bf16[512,512]{0,1:T(8,128)(2,1)}, f32[512,512]{0,1:T(8,128)S(1)}, bf16[1024,512]{1,0:T(8,128)(2,1)}, bf16[4,512,1024]{2,0,1:T(4,128)(2,1)}, bf...) conditional(s32[]{:T(128)} %convert_element_type.280, (bf16[4,4,128,512]{3,2,0,1:T(8,128)(2,1)}, ...), branch_computations={%region_10.28_spmd, %region_26.29_spmd} | conditional | flops 14625009664 | bytes 573496384 | solution.py:313
  228.3 4.7 copy.261
  233.0 4.2 reshape.451
  244.4 6.2 copy.263
  250.6 4.1 fusion.95
  254.7 3.2 fusion.99
  257.9 3.5 fusion.10
  263.8 3.8 fusion.26
  275.1 2.8 fusion.102
  280.6 4.6 reshape.466
  285.2 4.5 fusion.31
  289.7 4.5 copy.237
  294.2 6.1 pad_maximum_fusion
  308.5 8.0 %fusion.21 = bf16[8,64,1024]{2,1,0:T(8,128)(2,1)S(1)} fusion(bf16[512,8,64]{0,2,1:T(8,128)(2,1)S(1)} %bitcast.431, f32[8,512,1024]{2,1,0:T(8,128)} %copy-done.1, f32[8,512]{1,0:T(8,128)S(1)} %log_add_fusion), kind=kOutput, calls=%fused_computation.54 | convolution fusion | flops 545783808 | bytes 18366464 | tf_op jit(solution)/shard_map/cond/branch_0_fun/hqk,qhe->khe/dot_general | solution.py:149
  319.0 10.2 %multiply_reduce_fusion.2 = (f32[8,512]{1,0:T(8,128)}, f32[8,512,1024]{2,1,0:T(8,128)}) fusion(f32[8,512,1024]{2,1,0:T(8,128)S(1)} %bitcast.404, f32[8,512]{1,0:T(8,128)S(1)} %log_add_fusion, bf16[512,8,64]{0,2,1:T(8,128)(2,1)} %bitcast.432, bf16[1024,8,64]{0,2,1:T(8,128)(2,1)} %bitcast.477), kind=kOutput, calls=%fused_computation.29 | convolution fusion | flops 549449728 | bytes 35160064 | tf_op jit(solution)/shard_map/cond/branch_0_fun/qhe,khe->hqk/dot_general | solution.py:145
  329.3 10.2 %multiply_convert_fusion.1 = bf16[8,512,1024]{2,1,0:T(8,128)(2,1)} fusion(f32[8,512,1024]{2,1,0:T(8,128)} %get-tuple-element.419, f32[8,512,1024]{2,1,0:T(8,128)S(1)} %bitcast.404, f32[8,512]{1,0:T(8,128)} %get-tuple-element.418, f32[8,512]{1,0:T(8,128)S(1)} %log_add_fusion), kind=kLoop, calls=%fused_computation.28 | loop fusion | flops 16777216 | bytes 41975808 | tf_op jit(solution)/shard_map/cond/branch_0_fun/convert_element_type | solution.py:146
  339.4 6.5 %fusion.24 = bf16[8,64,512]{2,1,0:T(8,128)(2,1)S(1)} fusion(bf16[1024,8,64]{0,2,1:T(8,128)(2,1)} %bitcast.438, bf16[8,512,1024]{2,1,0:T(8,128)(2,1)} %multiply_convert_fusion.1), kind=kOutput, calls=%fused_computation.60 | convolution fusion | flops 537395200 | bytes 9961472 | tf_op jit(solution)/shard_map/cond/branch_0_fun/hqk,khe->qhe/dot_general | solution.py:147
  368.1 4.8 all-to-all-start.5
  372.9 4.1 copy.276
  377.0 3.1 copy.327
  380.1 3.7 gather_fusion.5
  383.8 14.4 %conditional.5 = (f32[512,512]{1,0:T(8,128)}, bf16[4,512,1024]{2,0,1:T(4,128)(2,1)}, f32[2,512]{1,0:T(2,128)S(1)}, f32[2,512]{1,0:T(2,128)S(1)}, bf16[512,512]{1,0:T(8,128)(2,1)S(1)}) conditional(s32[]{:T(128)} %convert_element_type.280, (f32[4,512]{1,0:T(4,128)S(1)}, f32[512,512]{0,1:T(8,128)S(1)}, bf16[4,512,1024]{2,0,1:T(4,128)(2,1)}) %tuple.159, ...), branch_computations={%region_27.30_spmd, %region_28.43_spmd} | conditional | flops 4320396288 | bytes 87687304 | solution.py:323
  399.9 7.6 %fusion.57 = bf16[8,64,1024]{2,1,0:T(8,128)(2,1)S(1)} fusion(bf16[512,8,64]{0,2,1:T(8,128)(2,1)S(1)} %bitcast.427, f32[8,512,1024]{2,1,0:T(8,128)} %copy-done, f32[8,512]{1,0:T(8,128)S(1)} %log_add_fusion.1), kind=kOutput, calls=%fused_computation.175 | convolution fusion | flops 545783808 | bytes 18366464 | tf_op jit(solution)/shard_map/hqk,qhe->khe/dot_general | solution.py:149
  407.5 13.7 %multiply_reduce_fusion.19 = (f32[8,512]{1,0:T(8,128)}, f32[8,512,1024]{2,1,0:T(8,128)}) fusion(f32[8,512,1024]{2,1,0:T(8,128)} %copy-done, f32[8,512]{1,0:T(8,128)S(1)} %log_add_fusion.1, bf16[512,8,64]{0,2,1:T(8,128)(2,1)S(1)} %bitcast.428, bf16[1024,8,64]{0,2,1:T(8,128)(2,1)} %bitcast.476), kind=kOutput, calls=%fused_computation.135 | convolution fusion | flops 549449728 | bytes 35160064 | tf_op jit(solution)/shard_map/qhe,khe->hqk/dot_general | solution.py:145
  421.2 10.3 %multiply_convert_fusion.6 = bf16[8,512,1024]{2,1,0:T(8,128)(2,1)} fusion(f32[8,512,1024]{2,1,0:T(8,128)} %get-tuple-element.464, f32[8,512,1024]{2,1,0:T(8,128)S(1)} %bitcast.402, f32[8,512]{1,0:T(8,128)} %get-tuple-element.463, f32[8,512]{1,0:T(8,128)S(1)} %log_add_fusion.1), kind=kLoop, calls=%fused_computation.134 | loop fusion | flops 16777216 | bytes 41975808 | tf_op jit(solution)/shard_map/convert_element_type | solution.py:146
  431.5 7.0 %fusion.60 = bf16[8,64,512]{2,1,0:T(8,128)(2,1)} fusion(bf16[1024,8,64]{0,2,1:T(8,128)(2,1)S(1)} %bitcast.437, bf16[8,512,1024]{2,1,0:T(8,128)(2,1)} %multiply_convert_fusion.6), kind=kOutput, calls=%fused_computation.182 | convolution fusion | flops 537395200 | bytes 9961472 | tf_op jit(solution)/shard_map/hqk,khe->qhe/dot_general | solution.py:147
  443.0 3.6 copy.325
  449.0 5.2 gather_fusion.4
  466.2 3.8 gather_fusion.3
  470.1 2.7 broadcast_select_fusion.1
  476.6 2.7 fusion.70
  482.1 4.8 all-to-all-start.6
  495.6 5.3 all-to-all-done.6
  500.9 3.5 all-to-all-start.7
  504.5 3.2 add_convert_fusion.12
  514.5 3.9 all-to-all-done.7
  518.3 4.2 all-to-all-start.9
  524.3 71.2 %reduce-scatter.4.cloned.1.call-done = f32[32,6]{1,0:T(8,128)} async-done(((f32[512,6]{1,0:T(8,128)}), f32[32,6]{1,0:T(8,128)}) %reduce-scatter.4.cloned.1.call-update) | async-done | bytes 784
  602.5 3.5 all-to-all-start.8
  615.3 16.4 %all-to-all-done.8 = bf16[4,128,1024]{2,1,0:T(8,128)(2,1)S(1)} async-done(((bf16[4,128,1024]{2,1,0:T(8,128)(2,1)}), bf16[4,128,1024]{2,1,0:T(8,128)(2,1)S(1)}, u32[]{:S(2)}, u32[]{:S(2)}) %all-to-all-start.8) | async-done | bytes 1048608 | tf_op jit(solution)/shard_map/all_to_all | solution.py:65
  (455 shorter events, 170.2 us)
Async XLA Ops:
  7.2 66.6 %collective-permute-start.5 = (s32[2,2,1024]{2,1,0:T(2,128)}, s32[2,2,1024]{2,1,0:T(2,128)S(1)}, u32[]{:S(2)}, u32[]{:S(2)}) collective-permute-start(s32[2,2,1024]{2,1,0:T(2,128)} %param.26), channel_id=1, source_target_pairs={{0,4},{4,0},{8,12},{12,8},{1,5},{5,1},{9,13},{13,9},{2,6},{6,2},{1... | collective-permute-start | bytes 49160 | tf_op jit(solution)/shard_map/ppermute | solution.py:15
  8.7 43.5 %collective-permute-start.9 = (bf16[128,4,64]{0,2,1:T(8,128)(2,1)S(1)}, bf16[128,4,64]{0,2,1:T(8,128)(2,1)S(1)}, u32[]{:S(2)}, u32[]{:S(2)}) collective-permute-start(bf16[128,4,64]{0,2,1:T(8,128)(2,1)S(1)} %pad_maximum_fusion.13), channel_id=1, source_target_pairs={{0,16},{16,0},{1,17},{17,1},{2,18},{18,2},{3,19},{19,3},{4,20},{20... | collective-permute-start | bytes 196616 | tf_op jit(solution)/shard_map/ppermute | solution.py:15
  10.7 41.4 %copy-start.78 = (bf16[1,128,512]{2,1,0:T(8,128)(2,1)S(1)}, bf16[1,128,512]{2,1,0:T(8,128)(2,1)}, u32[]{:S(2)}) copy-start(bf16[1,128,512]{2,1,0:T(8,128)(2,1)} %param.30) | copy-start | bytes 393220
  10.8 41.5 %copy-start.80 = (bf16[128,2,64]{0,2,1:T(8,128)(2,1)S(1)}, bf16[128,2,64]{0,2,1:T(8,128)(2,1)}, u32[]{:S(2)}) copy-start(bf16[128,2,64]{0,2,1:T(8,128)(2,1)} %param.35) | copy-start | bytes 98308
  10.8 41.5 %copy-start.81 = (bf16[64,128]{1,0:T(8,128)(2,1)S(1)}, bf16[64,128]{1,0:T(8,128)(2,1)}, u32[]{:S(2)}) copy-start(bf16[64,128]{1,0:T(8,128)(2,1)} %param.36) | copy-start | bytes 49156
  10.8 41.5 %copy-start.82 = (bf16[128,64]{0,1:T(8,128)(2,1)S(1)}, bf16[128,64]{0,1:T(8,128)(2,1)}, u32[]{:S(2)}) copy-start(bf16[128,64]{0,1:T(8,128)(2,1)} %param.34) | copy-start | bytes 49156
  11.6 40.8 %all-to-all-start.1 = ((bf16[4,128,512]{2,1,0:T(8,128)(2,1)}), bf16[4,128,512]{2,1,0:T(8,128)(2,1)S(1)}, u32[]{:S(2)}, u32[]{:S(2)}) async-start(bf16[4,128,512]{2,1,0:T(8,128)(2,1)} %broadcast_in_dim.93), calls=%async_computation.1 | async-start | bytes 1048576 | tf_op jit(solution)/shard_map/all_to_all | solution.py:30
  16.5 40.8 %copy-start.79 = (bf16[1,512,128]{2,1,0:T(8,128)(2,1)S(1)}, bf16[1,512,128]{2,1,0:T(8,128)(2,1)}, u32[]{:S(2)}) copy-start(bf16[1,512,128]{2,1,0:T(8,128)(2,1)} %param.31) | copy-start | bytes 393220
  16.5 40.9 %collective-permute-start = (bf16[2,128,512]{2,1,0:T(8,128)(2,1)S(1)}, bf16[2,128,512]{2,1,0:T(8,128)(2,1)S(1)}, u32[]{:S(2)}, u32[]{:S(2)}) collective-permute-start(bf16[2,128,512]{2,1,0:T(8,128)(2,1)S(1)} %get-tuple-element.445), channel_id=1, source_target_pairs={{0,4},{4,0},{8,12},{12,8},{1,5},{5,1},{9,13},{13,9},{2,6},{6,2},{1... | collective-permute-start | bytes 786440 | tf_op jit(solution)/shard_map/ppermute | solution.py:15
  18.1 77.6 %collective-permute-start.15 = (bf16[2,128,512]{2,1,0:T(8,128)(2,1)}, bf16[2,128,512]{2,1,0:T(8,128)(2,1)}, u32[]{:S(2)}, u32[]{:S(2)}) collective-permute-start(bf16[2,128,512]{2,1,0:T(8,128)(2,1)} %get-tuple-element.443), channel_id=1, source_target_pairs={{0,4},{4,0},{8,12},{12,8},{1,5},{5,1},{9,13},{13,9},{2,6},{6,2},{1... | collective-permute-start | bytes 786440 | tf_op jit(solution)/shard_map/ppermute | solution.py:15
  52.4 20.7 %copy-start.107 = (s32[4]{0:T(128)S(1)}, s32[4]{0:T(128)}, u32[]{:S(2)}) copy-start(s32[4]{0:T(128)} %constant.148.clone) | copy-start | bytes 52
  53.3 20.5 %copy-start.94 = (s32[2,2,1024]{2,1,0:T(2,128)S(1)}, s32[2,2,1024]{2,1,0:T(2,128)}, u32[]{:S(2)}) copy-start(s32[2,2,1024]{2,1,0:T(2,128)} %param.26) | copy-start | bytes 49156
  53.3 15.3 %all-to-all-start.3 = ((bf16[4,128,512]{2,1,0:T(8,128)(2,1)}), bf16[4,128,512]{2,1,0:T(8,128)(2,1)S(1)}, u32[]{:S(2)}, u32[]{:S(2)}) async-start(bf16[4,128,512]{2,1,0:T(8,128)(2,1)} %broadcast_in_dim.107), calls=%async_computation.3 | async-start | bytes 1048576 | tf_op jit(solution)/shard_map/all_to_all | solution.py:30
  57.4 59.1 %copy-start.92 = (f32[1,512]{1,0:T(1,128)}, f32[1,512]{1,0:T(1,128)S(1)}, u32[]{:S(2)}) copy-start(f32[1,512]{1,0:T(1,128)S(1)} %get-tuple-element.453) | copy-start | bytes 6148
  57.4 166.4 %copy-start.85 = (f32[3,512]{1,0:T(4,128)}, f32[3,512]{1,0:T(4,128)S(1)}, u32[]{:S(2)}) copy-start(f32[3,512]{1,0:T(4,128)S(1)} %get-tuple-element.452) | copy-start | bytes 18436
  57.4 166.4 %copy-start.87 = (f32[3,512]{1,0:T(4,128)}, f32[3,512]{1,0:T(4,128)S(1)}, u32[]{:S(2)}) copy-start(f32[3,512]{1,0:T(4,128)S(1)} %get-tuple-element.451) | copy-start | bytes 18436
  68.5 15.7 %all-to-all-start = ((bf16[4,128,512]{2,1,0:T(8,128)(2,1)}), bf16[4,128,512]{2,1,0:T(8,128)(2,1)S(1)}, u32[]{:S(2)}, u32[]{:S(2)}) async-start(bf16[4,128,512]{2,1,0:T(8,128)(2,1)} %maximum_select_fusion), calls=%async_computation | async-start | bytes 1048576 | tf_op jit(solution)/shard_map/all_to_all | solution.py:77
  73.6 63.6 %copy-start.100 = (pred[4]{0:T(512)(128)(4,1)}, pred[4]{0:T(512)(128)(4,1)S(1)}, u32[]{:S(2)}) copy-start(pred[4]{0:T(512)(128)(4,1)S(1)} %get-tuple-element.466) | copy-start | bytes 16
  73.6 60.0 %copy-start.98 = (s32[1024]{0:T(1024)}, s32[1024]{0:T(1024)S(1)}, u32[]{:S(2)}) copy-start(s32[1024]{0:T(1024)S(1)} %pad_clamp_fusion.1) | copy-start | bytes 12292
  85.3 32.7 %all-to-all-start.2 = ((bf16[4,128,1024]{2,1,0:T(8,128)(2,1)}), bf16[4,128,1024]{2,1,0:T(8,128)(2,1)S(1)}, u32[]{:S(2)}, u32[]{:S(2)}) async-start(bf16[4,128,1024]{2,1,0:T(8,128)(2,1)} %broadcast_in_dim.106), calls=%async_computation.2 | async-start | bytes 2097152 | tf_op jit(solution)/shard_map/all_to_all | solution.py:30
  89.9 10.3 %collective-permute-start.3 = (bf16[4,128,512]{2,1,0:T(8,128)(2,1)S(1)}, bf16[4,128,512]{2,1,0:T(8,128)(2,1)}, u32[]{:S(2)}, u32[]{:S(2)}) collective-permute-start(bf16[4,128,512]{2,1,0:T(8,128)(2,1)S(1)} %all-to-all-done.1), channel_id=1, source_target_pairs={{0,8},{4,12},{8,0},{12,4},{1,9},{5,13},{9,1},{13,5},{2,10},{6,14},... | collective-permute-start | bytes 1572872 | tf_op jit(solution)/shard_map/ppermute | solution.py:15
  90.8 20.7 %collective-permute-start.11 = (bf16[4,128,512]{2,1,0:T(8,128)(2,1)S(1)}, bf16[4,128,512]{2,1,0:T(8,128)(2,1)}, u32[]{:S(2)}, u32[]{:S(2)}) collective-permute-start(bf16[4,128,512]{2,1,0:T(8,128)(2,1)S(1)} %all-to-all-done.3), channel_id=1, source_target_pairs={{0,8},{4,12},{8,0},{12,4},{1,9},{5,13},{9,1},{13,5},{2,10},{6,14},... | collective-permute-start | bytes 1572872 | tf_op jit(solution)/shard_map/ppermute | solution.py:15
  91.5 24.2 %collective-permute-start.1 = (bf16[512,512]{1,0:T(8,128)(2,1)S(1)}, bf16[512,512]{1,0:T(8,128)(2,1)S(1)}, u32[]{:S(2)}, u32[]{:S(2)}) collective-permute-start(bf16[512,512]{1,0:T(8,128)(2,1)S(1)} %bitcast.408), channel_id=1, source_target_pairs={{0,4},{4,0},{8,12},{12,8},{1,5},{5,1},{9,13},{13,9},{2,6},{6,2},{1... | collective-permute-start | bytes 1572872 | tf_op jit(solution)/shard_map/ppermute | solution.py:15
  97.8 25.7 %collective-permute-start.2 = (bf16[4,128,512]{2,1,0:T(8,128)(2,1)S(1)}, bf16[4,128,512]{2,1,0:T(8,128)(2,1)}, u32[]{:S(2)}, u32[]{:S(2)}) collective-permute-start(bf16[4,128,512]{2,1,0:T(8,128)(2,1)S(1)} %all-to-all-done.1), channel_id=1, source_target_pairs={{0,4},{4,0},{8,12},{12,8},{1,5},{5,1},{9,13},{13,9},{2,6},{6,2},{1... | collective-permute-start | bytes 1572872 | tf_op jit(solution)/shard_map/ppermute | solution.py:15
  97.8 32.8 %collective-permute-start.10 = (bf16[4,128,512]{2,1,0:T(8,128)(2,1)S(1)}, bf16[4,128,512]{2,1,0:T(8,128)(2,1)}, u32[]{:S(2)}, u32[]{:S(2)}) collective-permute-start(bf16[4,128,512]{2,1,0:T(8,128)(2,1)S(1)} %all-to-all-done.3), channel_id=1, source_target_pairs={{0,4},{4,0},{8,12},{12,8},{1,5},{5,1},{9,13},{13,9},{2,6},{6,2},{1... | collective-permute-start | bytes 1572872 | tf_op jit(solution)/shard_map/ppermute | solution.py:15
  100.3 23.8 %collective-permute-start.4 = (bf16[4,128,512]{2,1,0:T(8,128)(2,1)}, bf16[4,128,512]{2,1,0:T(8,128)(2,1)}, u32[]{:S(2)}, u32[]{:S(2)}) collective-permute-start(bf16[4,128,512]{2,1,0:T(8,128)(2,1)} %collective-permute-done.3), channel_id=1, source_target_pairs={{0,4},{4,0},{8,12},{12,8},{1,5},{5,1},{9,13},{13,9},{2,6},{6,2},{1... | collective-permute-start | bytes 1572872 | tf_op jit(solution)/shard_map/ppermute | solution.py:15
  111.5 19.1 %collective-permute-start.12 = (bf16[4,128,512]{2,1,0:T(8,128)(2,1)}, bf16[4,128,512]{2,1,0:T(8,128)(2,1)}, u32[]{:S(2)}, u32[]{:S(2)}) collective-permute-start(bf16[4,128,512]{2,1,0:T(8,128)(2,1)} %collective-permute-done.11), channel_id=1, source_target_pairs={{0,4},{4,0},{8,12},{12,8},{1,5},{5,1},{9,13},{13,9},{2,6},{6,2},{1... | collective-permute-start | bytes 1572872 | tf_op jit(solution)/shard_map/ppermute | solution.py:15
  118.0 102.6 %all-to-all-start.4 = ((bf16[4,128,512]{2,1,0:T(8,128)(2,1)}), bf16[4,128,512]{2,1,0:T(8,128)(2,1)}, u32[]{:S(2)}, u32[]{:S(2)}) async-start(bf16[4,128,512]{2,1,0:T(8,128)(2,1)} %maximum_select_fusion.1), calls=%async_computation.4 | async-start | bytes 1048576 | tf_op jit(solution)/shard_map/all_to_all | solution.py:77
  122.6 35.4 %collective-permute-start.7 = (bf16[4,128,1024]{2,1,0:T(8,128)(2,1)S(1)}, bf16[4,128,1024]{2,1,0:T(8,128)(2,1)}, u32[]{:S(2)}, u32[]{:S(2)}) collective-permute-start(bf16[4,128,1024]{2,1,0:T(8,128)(2,1)S(1)} %all-to-all-done.2), channel_id=1, source_target_pairs={{0,8},{4,12},{8,0},{12,4},{1,9},{5,13},{9,1},{13,5},{2,10},{6,14},... | collective-permute-start | bytes 3145736 | tf_op jit(solution)/shard_map/ppermute | solution.py:15
  123.5 43.1 %collective-permute-start.6 = (bf16[4,128,1024]{2,1,0:T(8,128)(2,1)S(1)}, bf16[4,128,1024]{2,1,0:T(8,128)(2,1)}, u32[]{:S(2)}, u32[]{:S(2)}) collective-permute-start(bf16[4,128,1024]{2,1,0:T(8,128)(2,1)S(1)} %all-to-all-done.2), channel_id=1, source_target_pairs={{0,4},{4,0},{8,12},{12,8},{1,5},{5,1},{9,13},{13,9},{2,6},{6,2},{1... | collective-permute-start | bytes 3145736 | tf_op jit(solution)/shard_map/ppermute | solution.py:15
  158.0 8.6 %collective-permute-start.8 = (bf16[4,128,1024]{2,1,0:T(8,128)(2,1)}, bf16[4,128,1024]{2,1,0:T(8,128)(2,1)}, u32[]{:S(2)}, u32[]{:S(2)}) collective-permute-start(bf16[4,128,1024]{2,1,0:T(8,128)(2,1)} %collective-permute-done.7), channel_id=1, source_target_pairs={{0,4},{4,0},{8,12},{12,8},{1,5},{5,1},{9,13},{13,9},{2,6},{6,2},{1... | collective-permute-start | bytes 3145736 | tf_op jit(solution)/shard_map/ppermute | solution.py:15
  185.1 38.7 %copy-start.19 = (bf16[512,512]{0,1:T(8,128)(2,1)}, bf16[512,512]{0,1:T(8,128)(2,1)S(1)}, u32[]{:S(2)}) copy-start(bf16[512,512]{0,1:T(8,128)(2,1)S(1)} %get-tuple-element.133) | copy-start | bytes 1572868
  185.3 34.7 %collective-permute-start.13 = (bf16[512,512]{1,0:T(8,128)(2,1)S(1)}, bf16[512,512]{1,0:T(8,128)(2,1)S(1)}, u32[]{:S(2)}, u32[]{:S(2)}) collective-permute-start(bf16[512,512]{1,0:T(8,128)(2,1)S(1)} %copy.258), channel_id=1, source_target_pairs={{0,16},{1,17},{2,18},{3,19},{4,20},{5,21},{6,22},{7,23},{8,24},{9,... | collective-permute-start | bytes 1572872 | tf_op jit(solution)/shard_map/ppermute | solution.py:19
  220.0 2.7 collective-permute-start.14
  226.9 12.0 %copy-start.88 = (f32[512]{0:T(512)}, f32[512]{0:T(512)S(1)}, u32[]{:S(2)}) copy-start(f32[512]{0:T(512)S(1)} %broadcast_multiply_fusion.7) | copy-start | bytes 6148 | tf_op jit(solution)/shard_map/cond
  227.1 11.8 %copy-start.90 = (f32[512]{0:T(512)}, f32[512]{0:T(512)S(1)}, u32[]{:S(2)}) copy-start(f32[512]{0:T(512)S(1)} %add_rsqrt_fusion.3) | copy-start | bytes 6148 | tf_op jit(solution)/shard_map/cond
  227.1 11.8 %copy-start.102 = (f32[1,512]{1,0:T(1,128)}, f32[1,512]{1,0:T(1,128)S(1)}, u32[]{:S(2)}) copy-start(f32[1,512]{1,0:T(1,128)S(1)} %get-tuple-element.424) | copy-start | bytes 6148 | tf_op jit(solution)/shard_map/cond
  305.0 14.0 %slice-start.4 = ((s8[16777216]{0:T(1024)(128)(4,1)}), s8[4194304]{0:T(1024)(128)(4,1)S(1)}, s32[]{:S(2)}) async-start(s8[16777216]{0:T(1024)(128)(4,1)} %bitcast.403), calls=%async_computation.16 | async-start | bytes 8388608 | tf_op jit(solution)/shard_map/cond
  308.0 11.0 %slice-start.5 = ((s8[16777216]{0:T(1024)(128)(4,1)}), s8[4194304]{0:T(1024)(128)(4,1)S(1)}, s32[]{:S(2)}) async-start(s8[16777216]{0:T(1024)(128)(4,1)} %bitcast.403), calls=%async_computation.17 | async-start | bytes 8388608 | tf_op jit(solution)/shard_map/cond
  308.5 10.5 %slice-start.6 = ((s8[16777216]{0:T(1024)(128)(4,1)}), s8[4194304]{0:T(1024)(128)(4,1)S(1)}, s32[]{:S(2)}) async-start(s8[16777216]{0:T(1024)(128)(4,1)} %bitcast.403), calls=%async_computation.18 | async-start | bytes 8388608 | tf_op jit(solution)/shard_map/cond
  308.5 10.5 %slice-start.7 = ((s8[16777216]{0:T(1024)(128)(4,1)}), s8[4194304]{0:T(1024)(128)(4,1)S(1)}, s32[]{:S(2)}) async-start(s8[16777216]{0:T(1024)(128)(4,1)} %bitcast.403), calls=%async_computation.19 | async-start | bytes 8388608 | tf_op jit(solution)/shard_map/cond
  362.1 2.0 collective-permute-start.17
  362.9 17.2 %copy-start.97 = (s32[1024]{0:T(1024)}, s32[1024]{0:T(1024)S(1)}, u32[]{:S(2)}) copy-start(s32[1024]{0:T(1024)S(1)} %pad_clamp_fusion) | copy-start | bytes 12292
  365.0 18.7 %collective-permute-start.18 = (bf16[512,512]{1,0:T(8,128)(2,1)}, bf16[512,512]{1,0:T(8,128)(2,1)S(1)}, u32[]{:S(2)}, u32[]{:S(2)}) collective-permute-start(bf16[512,512]{1,0:T(8,128)(2,1)} %add_convert_fusion.18), channel_id=1, source_target_pairs={{16,0},{17,1},{18,2},{19,3},{20,4},{21,5},{22,6},{23,7},{24,8},{25... | collective-permute-start | bytes 1572872 | tf_op jit(solution)/shard_map/ppermute | solution.py:19
  368.1 114.1 %all-to-all-start.5 = ((bf16[4,128,512]{2,1,0:T(8,128)(2,1)}), bf16[4,128,512]{2,1,0:T(8,128)(2,1)}, u32[]{:S(2)}, u32[]{:S(2)}) async-start(bf16[4,128,512]{2,1,0:T(8,128)(2,1)} %bitcast.139), calls=%async_computation.5 | async-start | bytes 1048576 | tf_op jit(solution)/shard_map/all_to_all | solution.py:83
  399.9 21.3 %slice-start = ((s8[16777216]{0:T(1024)(128)(4,1)}), s8[4194304]{0:T(1024)(128)(4,1)S(1)}, s32[]{:S(2)}) async-start(s8[16777216]{0:T(1024)(128)(4,1)} %bitcast.401), calls=%async_computation.12 | async-start | bytes 8388608
  399.9 21.3 %slice-start.1 = ((s8[16777216]{0:T(1024)(128)(4,1)}), s8[4194304]{0:T(1024)(128)(4,1)S(1)}, s32[]{:S(2)}) async-start(s8[16777216]{0:T(1024)(128)(4,1)} %bitcast.401), calls=%async_computation.13 | async-start | bytes 8388608
  407.5 13.7 %slice-start.2 = ((s8[16777216]{0:T(1024)(128)(4,1)}), s8[4194304]{0:T(1024)(128)(4,1)S(1)}, s32[]{:S(2)}) async-start(s8[16777216]{0:T(1024)(128)(4,1)} %bitcast.401), calls=%async_computation.14 | async-start | bytes 8388608
  407.5 13.7 %slice-start.3 = ((s8[16777216]{0:T(1024)(128)(4,1)}), s8[4194304]{0:T(1024)(128)(4,1)S(1)}, s32[]{:S(2)}) async-start(s8[16777216]{0:T(1024)(128)(4,1)} %bitcast.401), calls=%async_computation.15 | async-start | bytes 8388608
  459.4 45.0 %collective-permute-start.23 = (bf16[2,4,128,1024]{3,2,1,0:T(8,128)(2,1)}, bf16[2,4,128,1024]{3,2,1,0:T(8,128)(2,1)}, u32[]{:S(2)}, u32[]{:S(2)}) collective-permute-start(bf16[2,4,128,1024]{3,2,1,0:T(8,128)(2,1)} %slice.386), channel_id=1, source_target_pairs={{0,4},{4,0},{8,12},{12,8},{1,5},{5,1},{9,13},{13,9},{2,6},{6,2},{1... | collective-permute-start | bytes 6291464 | tf_op jit(solution)/shard_map/ppermute | solution.py:15
  464.5 10.5 %collective-permute-start.19 = (bf16[512,512]{1,0:T(8,128)(2,1)S(1)}, bf16[512,512]{1,0:T(8,128)(2,1)S(1)}, u32[]{:S(2)}, u32[]{:S(2)}) collective-permute-start(bf16[512,512]{1,0:T(8,128)(2,1)S(1)} %slice.479), channel_id=1, source_target_pairs={{0,4},{4,0},{8,12},{12,8},{1,5},{5,1},{9,13},{13,9},{2,6},{6,2},{1... | collective-permute-start | bytes 1572872 | tf_op jit(solution)/shard_map/ppermute | solution.py:15
  474.5 4.8 collective-permute-start.21
  475.0 14.1 %collective-permute-start.25 = (bf16[2,4,128,512]{3,2,1,0:T(8,128)(2,1)}, bf16[2,4,128,512]{3,2,1,0:T(8,128)(2,1)}, u32[]{:S(2)}, u32[]{:S(2)}) collective-permute-start(bf16[2,4,128,512]{3,2,1,0:T(8,128)(2,1)} %slice.396), channel_id=1, source_target_pairs={{0,4},{4,0},{8,12},{12,8},{1,5},{5,1},{9,13},{13,9},{2,6},{6,2},{1... | collective-permute-start | bytes 3145736 | tf_op jit(solution)/shard_map/ppermute | solution.py:15
  481.5 13.2 %collective-permute-start.22 = (bf16[1,4,128,512]{3,2,1,0:T(8,128)(2,1)}, bf16[1,4,128,512]{3,2,1,0:T(8,128)(2,1)S(1)}, u32[]{:S(2)}, u32[]{:S(2)}) collective-permute-start(bf16[1,4,128,512]{3,2,1,0:T(8,128)(2,1)} %slice.382), channel_id=1, source_target_pairs={{0,8},{4,12},{8,0},{12,4},{1,9},{5,13},{9,1},{13,5},{2,10},{6,14},... | collective-permute-start | bytes 1572872 | tf_op jit(solution)/shard_map/ppermute | solution.py:15
  482.1 18.8 %all-to-all-start.6 = ((bf16[4,128,512]{2,1,0:T(8,128)(2,1)}), bf16[4,128,512]{2,1,0:T(8,128)(2,1)S(1)}, u32[]{:S(2)}, u32[]{:S(2)}) async-start(bf16[4,128,512]{2,1,0:T(8,128)(2,1)} %bitcast.151), calls=%async_computation.6 | async-start | bytes 1048576 | tf_op jit(solution)/shard_map/all_to_all | solution.py:83
  488.0 21.6 %collective-permute-start.16 = (bf16[2,128,512]{2,1,0:T(8,128)(2,1)S(1)}, bf16[2,128,512]{2,1,0:T(8,128)(2,1)}, u32[]{:S(2)}, u32[]{:S(2)}) collective-permute-start(bf16[2,128,512]{2,1,0:T(8,128)(2,1)S(1)} %broadcast_select_fusion.10), channel_id=1, source_target_pairs={{0,4},{4,0},{8,12},{12,8},{1,5},{5,1},{9,13},{13,9},{2,6},{6,2},{1... | collective-permute-start | bytes 786440 | tf_op jit(solution)/shard_map/ppermute | solution.py:15
  491.5 20.8 %collective-permute-start.26 = (bf16[1,4,128,512]{3,2,1,0:T(8,128)(2,1)}, bf16[1,4,128,512]{3,2,1,0:T(8,128)(2,1)}, u32[]{:S(2)}, u32[]{:S(2)}) collective-permute-start(bf16[1,4,128,512]{3,2,1,0:T(8,128)(2,1)} %slice.398), channel_id=1, source_target_pairs={{0,8},{4,12},{8,0},{12,4},{1,9},{5,13},{9,1},{13,5},{2,10},{6,14},... | collective-permute-start | bytes 1572872 | tf_op jit(solution)/shard_map/ppermute | solution.py:15
  500.9 17.4 %all-to-all-start.7 = ((bf16[4,128,512]{2,1,0:T(8,128)(2,1)}), bf16[4,128,512]{2,1,0:T(8,128)(2,1)S(1)}, u32[]{:S(2)}, u32[]{:S(2)}) async-start(bf16[4,128,512]{2,1,0:T(8,128)(2,1)} %fusion.77), calls=%async_computation.7 | async-start | bytes 1048576 | tf_op jit(solution)/shard_map/all_to_all | solution.py:65
  504.4 91.1 %reduce-scatter.4.cloned.1.call-start = ((), (), s32[]{:S(2)}) async-start(), calls=%async_computation.11 | async-start | bytes 278528
  508.7 91.2 %collective-permute-start.24 = (bf16[1,4,128,1024]{3,2,1,0:T(8,128)(2,1)}, bf16[1,4,128,1024]{3,2,1,0:T(8,128)(2,1)}, u32[]{:S(2)}, u32[]{:S(2)}) collective-permute-start(bf16[1,4,128,1024]{3,2,1,0:T(8,128)(2,1)} %slice.388), channel_id=1, source_target_pairs={{0,8},{4,12},{8,0},{12,4},{1,9},{5,13},{9,1},{13,5},{2,10},{6,14},... | collective-permute-start | bytes 3145736 | tf_op jit(solution)/shard_map/ppermute | solution.py:15
  518.3 84.2 %all-to-all-start.9 = ((bf16[4,128,512]{2,1,0:T(8,128)(2,1)}), bf16[4,128,512]{2,1,0:T(8,128)(2,1)}, u32[]{:S(2)}, u32[]{:S(2)}) async-start(bf16[4,128,512]{2,1,0:T(8,128)(2,1)} %fusion.78), calls=%async_computation.9 | async-start | bytes 1048576 | tf_op jit(solution)/shard_map/all_to_all | solution.py:65
  597.3 10.5 %collective-permute-start.20 = (bf16[2,128,512]{2,1,0:T(8,128)(2,1)}, bf16[2,128,512]{2,1,0:T(8,128)(2,1)S(1)}, u32[]{:S(2)}, u32[]{:S(2)}) collective-permute-start(bf16[2,128,512]{2,1,0:T(8,128)(2,1)} %broadcast_select_fusion.6), channel_id=1, source_target_pairs={{0,4},{4,0},{8,12},{12,8},{1,5},{5,1},{9,13},{13,9},{2,6},{6,2},{1... | collective-permute-start | bytes 786440 | tf_op jit(solution)/shard_map/ppermute | solution.py:15
  602.5 29.2 %all-to-all-start.8 = ((bf16[4,128,1024]{2,1,0:T(8,128)(2,1)}), bf16[4,128,1024]{2,1,0:T(8,128)(2,1)S(1)}, u32[]{:S(2)}, u32[]{:S(2)}) async-start(bf16[4,128,1024]{2,1,0:T(8,128)(2,1)} %fusion.74), calls=%async_computation.8 | async-start | bytes 2097152 | tf_op jit(solution)/shard_map/all_to_all | solution.py:65
  610.0 4.0 collective-permute-start.27
  (88 other events, 358.6 us)
Sparse Core Ops, SparseCore 0:
  512.4 83.0 reduce-scatter.3
